TPU v7x, 128 devices: a whole 4x4x4 slice. The times are simulated.
128 devices in a mesh: section: 4 (over z), dp: 32 (over y, x, core).
Axes of the slice: x: 4, y: 4, z: 4, core: 2. Of those that a mesh axis runs over, the one named last changes fastest.
Arguments:
- h_saved: bfloat16 [2, 4, 128, 8, 19, 384], P(None, 'section', 'dp'), may hold values from -6 to 6
- out_cot: bfloat16 [128, 8, 19, 384], P('dp'), may hold values from -6 to 6
- so2_weight: bfloat16 [2, 4, 5, 384, 384], P(None, 'section'), may hold values from -0.3125 to 0.3125
- radial: bfloat16 [128, 112, 384], P('dp'), may hold values from 0.049804688 to 0.5
- edge_angle: float32 [128, 112], P('dp'), may hold values from -3.140625 to 3.140625
- edge_atoms: int32 [128, 2, 112], P('dp'), may hold values from 0 to 7, as said below
- edge_count: int32 [128], P('dp'), may hold values from 56 to 112
- atom_count: int32 [128], P('dp'), may hold values from 4 to 8
Outputs:
- in_grad: bfloat16 [128, 8, 19, 384], P('dp', 'section')
- weight_grad: float32 [2, 4, 5, 384, 384], P(None, 'section', None, 'dp')
Inputs may be any that keep to these rules, and one draw needn't show every extreme that they name: `edge_atoms`: in micro-batch b both atoms of every edge slot are below atom_count[b]; slots from edge_count[b] on are padding.
All inputs are finite; a program needn't handle non-finite values.
Results may differ from a plain program's by a relative error of at most 0.015.
Values may be sent and summed in bfloat16 or wider, within the bound.
A program may use at most 128 MiB of HBM per device.

v0:
```python
import math

import jax
import jax.numpy as jnp
from jax import lax
from jax.sharding import PartitionSpec as P


def edge_tables(radial, edge_angle, edge_atoms, edge_count):
    batches, edges = edge_angle.shape
    atoms = 8
    ids = jnp.arange(atoms, dtype=jnp.int32)
    to_dst = (edge_atoms[:, 0, :, None] == ids).astype(jnp.float32)
    to_src = (edge_atoms[:, 1, :, None] == ids).astype(jnp.float32)
    valid = (jnp.arange(edges, dtype=jnp.int32)[None] < edge_count[:, None]).astype(jnp.float32)
    trig = jnp.stack(
        [
            jnp.ones_like(edge_angle),
            jnp.cos(edge_angle),
            jnp.sin(edge_angle),
            jnp.cos(2.0 * edge_angle),
            jnp.sin(2.0 * edge_angle),
        ],
        1,
    ) * (0.25 * valid[:, None])
    pick = trig[:, :, None, None, :] * (
        to_dst.transpose(0, 2, 1)[:, None, :, None, :] * to_src.transpose(0, 2, 1)[:, None, None, :, :]
    )
    pick_hi = pick.astype(jnp.bfloat16)
    pick_lo = (pick - pick_hi.astype(jnp.float32)).astype(jnp.bfloat16)
    both = jnp.concatenate([pick_hi, pick_lo], -1)
    twice = jnp.concatenate([radial, radial], 1)
    return jnp.einsum("btdse,bec->btdsc", both, twice, preferred_element_type=jnp.float32)


def complex_mix(rows, real, imag):
    plus, minus = rows[..., 0, :, :], rows[..., 1, :, :]
    both = jnp.concatenate(
        [jnp.concatenate([plus, -minus], -1), jnp.concatenate([minus, plus], -1)], -2
    )
    out = jnp.einsum(
        "...kc,cd->...kd", both, jnp.concatenate([real, imag], 0), preferred_element_type=jnp.float32
    )
    half = out.shape[-2] // 2
    return out[..., :half, :], out[..., half:, :]


def body(h_saved, out_cot, so2_weight, radial, edge_angle, edge_atoms, edge_count, atom_count):
    groups = lax.axis_size("section")
    group_index = lax.axis_index("section")
    batches, atoms, rows, channels = out_cot.shape
    table = edge_tables(radial, edge_angle, edge_atoms, edge_count)
    h = h_saved[:, 0].transpose(0, 1, 3, 2, 4)
    w = so2_weight[:, 0]
    spans = ((5, 9, 13, 1, 4), (13, 16, 19, 3, 3))

    def aggregate(values, forward):
        def apply(t, v):
            total = 0.0
            for n in range(atoms):
                tab = t[:, :, n] if forward else t[:, n]
                total = total + tab[:, None] * v[:, :, n : n + 1]
            return total

        parts = [apply(table[:, 0], values[:, 0:5])]
        for low, mid, high, slot, _ in spans:
            p, m = values[:, low:mid], values[:, mid:high]
            c, q = table[:, slot], table[:, slot + 1]
            if forward:
                parts += [apply(c, p) + apply(q, m), apply(c, m) - apply(q, p)]
            else:
                parts += [apply(c, p) - apply(q, m), apply(q, p) + apply(c, m)]
        return parts

    def forward(r):
        hr = h[r]
        out = [
            jnp.dot(hr[:, 0:5].reshape(-1, channels), w[r, 0], preferred_element_type=jnp.float32).reshape(
                batches, 5, atoms, channels
            )
        ]
        for low, mid, high, slot, k in spans:
            pair = hr[:, low:high].reshape(batches, 2, k * atoms, channels)
            p, m = complex_mix(pair, w[r, slot], w[r, slot + 1])
            out += [p.reshape(batches, k, atoms, channels), m.reshape(batches, k, atoms, channels)]
        return jnp.concatenate(aggregate(jnp.concatenate(out, 1), True), 1)

    summed = [forward(r) for r in range(2)]
    gates = [jax.nn.sigmoid(s[:, 0]) for s in summed]

    def backward(r, g):
        gf = g.astype(jnp.float32)
        gate = gates[r]
        d = gf * gate[:, None]
        extra = jnp.sum(gf * summed[r], 1) * gate * (1.0 - gate)
        d = jnp.concatenate([d[:, 0:1] + extra[:, None], d[:, 1:]], 1)
        parts = [x.astype(jnp.bfloat16) for x in aggregate(d, False)]
        nt = (((1,), (1,)), ((), ()))
        tn = (((0,), (0,)), ((), ()))
        hr = h[r]
        u0 = parts[0].reshape(-1, channels)
        back = [
            lax.dot_general(u0, w[r, 0], nt, preferred_element_type=jnp.float32).reshape(
                batches, 5, atoms, channels
            )
        ]
        grads = [lax.dot_general(hr[:, 0:5].reshape(-1, channels), u0, tn, preferred_element_type=jnp.float32)]
        for n, (low, mid, high, slot, k) in enumerate(spans):
            up = parts[1 + 2 * n].reshape(-1, channels)
            um = parts[2 + 2 * n].reshape(-1, channels)
            bar = jnp.concatenate([jnp.concatenate([up, um], 1), jnp.concatenate([um, -up], 1)], 0)
            wt = jnp.concatenate([w[r, slot], w[r, slot + 1]], 1)
            out = lax.dot_general(bar, wt, nt, preferred_element_type=jnp.float32)
            out = out.reshape(2, batches, k, atoms, channels)
            back += [out[0], out[1]]
            pair = jnp.concatenate(
                [hr[:, low:mid].reshape(-1, channels), hr[:, mid:high].reshape(-1, channels)], 0
            )
            dw = lax.dot_general(pair, bar, tn, preferred_element_type=jnp.float32)
            grads += [dw[:, :channels], dw[:, channels:]]
        return (gf + jnp.concatenate(back, 1)).astype(jnp.bfloat16), jnp.stack(grads)

    start = out_cot.transpose(0, 2, 1, 3)
    g = start
    weight_grads = []
    kept = []
    perm = [(i, (i - 1) % groups) for i in range(groups)]
    for lap in (1, 0):
        mine = None
        for step in range(groups):
            active = group_index == groups - 1 - step
            g, grads = lax.cond(
                active,
                lambda v: backward(lap, v),
                lambda v: (v, jnp.zeros((5, channels, channels), jnp.float32)),
                g,
            )
            mine = grads if mine is None else jnp.where(active, grads, mine)
            if not (lap == 0 and step == groups - 1):
                g = lax.ppermute(g, "section", perm)
        weight_grads.append(mine)
    norm_scale = 1.0 / math.sqrt(lax.axis_size("dp") * batches * edge_angle.shape[1])
    total = jnp.stack(weight_grads[::-1]) * norm_scale
    total = lax.psum_scatter(total, "dp", scatter_dimension=2, tiled=True)
    live = (jnp.arange(atoms, dtype=jnp.int32)[None, :] < atom_count[:, None])[:, None, :, None]
    g = jnp.where(live & (group_index == 0), g, jnp.zeros_like(g)).transpose(0, 2, 1, 3)
    share = atoms // groups
    own = lax.psum_scatter(g, "section", scatter_dimension=1, tiled=True)
    return own, total[:, None]


def solution(mesh):
    placed = (
        P(None, "section", "dp", None, None, None),
        P("dp", None, None, None),
        P(None, "section", None, None, None),
        P("dp", None, None),
        P("dp", None),
        P("dp", None, None),
        P("dp"),
        P("dp"),
    )
    return jax.shard_map(
        body,
        mesh=mesh,
        in_specs=placed,
        out_specs=(P("dp", "section", None, None), P(None, "section", None, "dp", None)),
        check_vma=False,
    )
```

profile of v0, /device:TPU:1, one launch (start us, length us, event | category | flops | bytes accessed | tf_op | source)
XLA Modules:
  0.0 423.5 jit_solution(8502944646664391287)
XLA Ops:
  7.2 2.2 slice_bitcast_fusion.432
  12.4 1.5 slice_bitcast_fusion.440
  18.0 0.9 constant_dynamic-update-slice_fusion.37
  20.9 1.1 add_dynamic-update-slice_fusion.1
  22.1 1.1 subtract_dynamic-update-slice_fusion.1
  23.1 0.9 add_dynamic-update-slice_fusion.3
  24.2 0.9 subtract_dynamic-update-slice_fusion.3
  25.1 2.2 conditional.8
  25.1 1.8 broadcast.1273.clone
  27.3 19.3 %collective-permute-start = (bf16[4,19,8,384]{3,2,1,0:T(8,128)(2,1)S(1)}, bf16[4,19,8,384]{3,2,1,0:T(8,128)(2,1)}, u32[]{:S(2)}, u32[]{:S(2)}) collective-permute-start(bf16[4,19,8,384]{3,2,1,0:T(8,128)(2,1)S(1)} %get-tuple-element.170), channel_id=1, source_target_pairs={{0,96},{32,0},{64,32},{96,64},{1,97},{33,1},{65,33},{97,65},{2,98}... | collective-permute-start | bytes 1400840 | tf_op jit(solution)/shard_map/ppermute | solution.py:140
  46.6 1.9 fusion.274
  48.5 0.9 slice.5177
  49.5 1.0 slice.5154
  53.1 2.3 fusion.364
  60.4 1.5 fusion.256
  81.9 2.0 conditional.9
  81.9 1.8 broadcast.1275.clone
  84.0 2.0 constant_dynamic-update-slice_fusion.38
  86.0 1.5 add_dynamic-update-slice_fusion
  87.5 7.9 %collective-permute-done.1 = bf16[4,19,8,384]{3,2,1,0:T(8,128)(2,1)S(1)} collective-permute-done((bf16[4,19,8,384]{3,2,1,0:T(8,128)(2,1)}, bf16[4,19,8,384]{3,2,1,0:T(8,128)(2,1)S(1)}, u32[]{:S(2)}, u32[]{:S(2)}) %collective-permute-start.1) | collective-permute-done | bytes 466976 | tf_op jit(solution)/shard_map/ppermute | solution.py:140
  95.5 1.8 conditional.10
  95.5 1.8 broadcast.1277.clone
  98.0 1.5 collective-permute-start.2
  99.5 2.2 subtract_dynamic-update-slice_fusion
  101.8 2.2 add_dynamic-update-slice_fusion.2
  104.0 19.9 %collective-permute-done.2 = bf16[4,19,8,384]{3,2,1,0:T(8,128)(2,1)S(1)} collective-permute-done((bf16[4,19,8,384]{3,2,1,0:T(8,128)(2,1)}, bf16[4,19,8,384]{3,2,1,0:T(8,128)(2,1)S(1)}, u32[]{:S(2)}, u32[]{:S(2)}) %collective-permute-start.2) | collective-permute-done | bytes 466976 | tf_op jit(solution)/shard_map/ppermute | solution.py:140
  123.8 17.8 %conditional.11 = (bf16[4,19,8,384]{3,2,1,0:T(8,128)(2,1)S(1)}, f32[5,384,384]{2,1,0:T(8,128)}) conditional(s32[]{:T(128)} %convert_element_type.259, bf16[4,19,8,384]{3,2,1,0:T(8,128)(2,1)S(1)} %collective-permute-done.2, (bf16[4,19,8,384]{3,2,1,0:T(8,128)(2,1)S(1)}, f32[4,5,8,8,384]{4,3,2,1,0:T(8,128)S(1)}, f32[4,8,384]{2,1,0:T(8,128)S(1)}, ...), branch_computations={%region_9.10_spmd, %region_10.12_spmd} | conditional | flops 639713280 | bytes 61268012 | solution.py:132
  124.3 1.3 fusion.91
  127.0 0.8 copy-done.5
  132.2 1.2 fusion.90
  133.3 0.9 fusion.96
  135.0 0.9 fusion.94
  135.9 0.9 fusion.93
  136.8 4.8 %copy.1854 = f32[5,384,384]{2,1,0:T(8,128)} copy(f32[5,384,384]{1,2,0:T(8,128)} %fusion.93) | data formatting | bytes 5898240 | tf_op jit(solution)/shard_map/cond | solution.py:132
  143.3 2.1 subtract_dynamic-update-slice_fusion.2
  145.4 7.4 %collective-permute-done.3 = bf16[4,19,8,384]{3,2,1,0:T(8,128)(2,1)S(1)} collective-permute-done((bf16[4,19,8,384]{3,2,1,0:T(8,128)(2,1)}, bf16[4,19,8,384]{3,2,1,0:T(8,128)(2,1)S(1)}, u32[]{:S(2)}, u32[]{:S(2)}) %collective-permute-start.3) | collective-permute-done | bytes 466976 | tf_op jit(solution)/shard_map/ppermute | solution.py:140
  152.8 1.8 conditional.12
  152.8 1.8 broadcast.1281.clone
  154.6 17.2 %collective-permute-start.4 = (bf16[4,19,8,384]{3,2,1,0:T(8,128)(2,1)S(1)}, bf16[4,19,8,384]{3,2,1,0:T(8,128)(2,1)}, u32[]{:S(2)}, u32[]{:S(2)}) collective-permute-start(bf16[4,19,8,384]{3,2,1,0:T(8,128)(2,1)S(1)} %get-tuple-element.174), channel_id=1, source_target_pairs={{0,96},{32,0},{64,32},{96,64},{1,97},{33,1},{65,33},{97,65},{2,98}... | collective-permute-start | bytes 1400840 | tf_op jit(solution)/shard_map/ppermute | solution.py:140
  171.9 7.4 %collective-permute-done.4 = bf16[4,19,8,384]{3,2,1,0:T(8,128)(2,1)} collective-permute-done((bf16[4,19,8,384]{3,2,1,0:T(8,128)(2,1)S(1)}, bf16[4,19,8,384]{3,2,1,0:T(8,128)(2,1)}, u32[]{:S(2)}, u32[]{:S(2)}) %collective-permute-start.4) | collective-permute-done | bytes 466976 | tf_op jit(solution)/shard_map/ppermute | solution.py:140
  179.2 1.8 conditional.13
  179.2 1.8 broadcast.1283.clone
  181.1 3.5 collective-permute-start.5
  184.6 6.7 %collective-permute-done.5 = bf16[4,19,8,384]{3,2,1,0:T(8,128)(2,1)S(1)} collective-permute-done((bf16[4,19,8,384]{3,2,1,0:T(8,128)(2,1)}, bf16[4,19,8,384]{3,2,1,0:T(8,128)(2,1)S(1)}, u32[]{:S(2)}, u32[]{:S(2)}) %collective-permute-start.5) | collective-permute-done | bytes 466976 | tf_op jit(solution)/shard_map/ppermute | solution.py:140
  191.3 1.8 conditional.14
  191.3 1.8 broadcast.1285.clone
  193.9 16.9 %collective-permute-start.6 = (bf16[4,19,8,384]{3,2,1,0:T(8,128)(2,1)}, bf16[4,19,8,384]{3,2,1,0:T(8,128)(2,1)S(1)}, u32[]{:S(2)}, u32[]{:S(2)}) collective-permute-start(bf16[4,19,8,384]{3,2,1,0:T(8,128)(2,1)} %copy-done.16), channel_id=1, source_target_pairs={{0,96},{32,0},{64,32},{96,64},{1,97},{33,1},{65,33},{97,65},{2,98}... | collective-permute-start | bytes 1400840 | tf_op jit(solution)/shard_map/ppermute | solution.py:140
  210.9 5.0 %select_bitcast_fusion = f32[1,5,384,384]{3,2,1,0:T(8,128)} fusion(f32[5,384,384]{2,1,0:T(8,128)} %get-tuple-element.387, f32[5,384,384]{2,1,0:T(8,128)} %get-tuple-element.386, f32[5,384,384]{2,1,0:T(8,128)} %get-tuple-element.385, f32[5,384,384]{2,1,0:T(8,128)} %get-tuple-element.384, pred[]{:T(512)S(6)} %eq.59, pred[]{:T(512)S(6)} %eq.58, pred[]{:T(512)S(6)} %eq.57), kind=kLoop, calls=%fused_computation.1209 | loop fusion | flops 2211840 | bytes 14745603 | tf_op jit(solution)/shard_map/stack | solution.py:143
  215.9 18.1 %collective-permute-done.6 = bf16[4,19,8,384]{3,2,1,0:T(8,128)(2,1)S(1)} collective-permute-done((bf16[4,19,8,384]{3,2,1,0:T(8,128)(2,1)}, bf16[4,19,8,384]{3,2,1,0:T(8,128)(2,1)S(1)}, u32[]{:S(2)}, u32[]{:S(2)}) %collective-permute-start.6) | collective-permute-done | bytes 466976 | tf_op jit(solution)/shard_map/ppermute | solution.py:140
  234.0 15.2 %conditional.15 = (bf16[4,19,8,384]{3,2,1,0:T(8,128)(2,1)S(1)}, f32[5,384,384]{2,1,0:T(8,128)}) conditional(s32[]{:T(128)} %convert_element_type.259, bf16[4,19,8,384]{3,2,1,0:T(8,128)(2,1)S(1)} %collective-permute-done.6, (bf16[4,19,8,384]{3,2,1,0:T(8,128)(2,1)S(1)}, f32[4,5,8,8,384]{4,3,2,1,0:T(8,128)S(1)}, f32[4,8,384]{2,1,0:T(8,128)S(1)}, ...), branch_computations={%region_21.22_spmd, %region_22.24_spmd} | conditional | flops 639713280 | bytes 49471504 | solution.py:132
  239.8 1.1 fusion.210
  240.9 0.9 fusion.216
  241.8 0.9 fusion.215
  242.7 0.9 fusion.214
  243.5 0.8 fusion.213
  244.4 4.8 %copy.1862 = f32[5,384,384]{2,1,0:T(8,128)} copy(f32[5,384,384]{1,2,0:T(8,128)} %fusion.213) | data formatting | bytes 5898240 | tf_op jit(solution)/shard_map/cond | solution.py:132
  249.2 1.1 fusion.259
  250.6 3.4 select_bitcast_fusion.1
  254.7 7.0 %copy.1678 = f32[2,5,384,384]{3,0,1,2:T(2,128)} copy(f32[2,5,384,384]{3,2,1,0:T(8,128)S(1)} %maximum_multiply_fusion) | data formatting | bytes 11796480 | tf_op jit(solution)/shard_map/mul | solution.py:143
  264.8 29.3 %all-reduce.5.cloned.1.call-done = bf16[4,8,19,384]{3,0,2,1:T(4,128)(2,1)} async-done(((bf16[4,8,19,384]{3,0,2,1:T(4,128)(2,1)}), bf16[4,8,19,384]{3,0,2,1:T(4,128)(2,1)}) %all-reduce.5.cloned.1.call-update) | async-done | bytes 466960
  294.1 0.9 constant_dynamic-slice_fusion
  295.8 118.8 %all-reduce.7.cloned.1.call-done = f32[2,5,384,384]{3,0,1,2:T(2,128)} async-done(((f32[2,5,384,384]{3,0,1,2:T(2,128)}), f32[2,5,384,384]{3,0,1,2:T(2,128)}) %all-reduce.7.cloned.1.call-update) | async-done | bytes 5898256
  414.6 1.0 dynamic-slice_bitcast_fusion
  415.6 0.9 copy.1681
  (457 shorter events, 53.6 us)
Async XLA Ops:
  7.2 5.0 %copy-start.9 = (bf16[2,1,4,8,19,384]{5,3,4,2,1,0:T(8,128)(2,1)S(1)}, bf16[2,1,4,8,19,384]{5,3,4,2,1,0:T(8,128)(2,1)}, u32[]{:S(2)}) copy-start(bf16[2,1,4,8,19,384]{5,3,4,2,1,0:T(8,128)(2,1)} %param.24) | copy-start | bytes 2801668
  7.2 286.9 %all-reduce.5.cloned.1.call-start = ((), (), s32[]{:S(2)}) async-start(), calls=%async_computation | async-start | bytes 933888
  7.2 4.9 %copy-start = (bf16[2,1,5,384,384]{4,3,2,1,0:T(8,128)(2,1)S(1)}, bf16[2,1,5,384,384]{4,3,2,1,0:T(8,128)(2,1)}, u32[]{:S(2)}) copy-start(bf16[2,1,5,384,384]{4,3,2,1,0:T(8,128)(2,1)} %param.26) | copy-start | bytes 8847364
  11.5 2.5 copy-start.76
  11.5 2.6 copy-start.75
  11.5 2.6 copy-start.74
  12.4 2.5 copy-start.57
  15.9 8.1 %copy-start.31 = (f32[4,8,1,384]{3,1,2,0:T(8,128)}, f32[4,8,1,384]{3,1,2,0:T(8,128)S(1)}, u32[]{:S(2)}) copy-start(f32[4,8,1,384]{3,1,2,0:T(8,128)S(1)} %copy.2609) | copy-start | bytes 147460
  16.0 8.1 %copy-start.33 = (f32[4,8,1,384]{3,1,2,0:T(8,128)}, f32[4,8,1,384]{3,1,2,0:T(8,128)S(1)}, u32[]{:S(2)}) copy-start(f32[4,8,1,384]{3,1,2,0:T(8,128)S(1)} %copy.2602) | copy-start | bytes 147460
  16.0 8.0 %copy-start.35 = (f32[4,8,1,384]{3,1,2,0:T(8,128)}, f32[4,8,1,384]{3,1,2,0:T(8,128)S(1)}, u32[]{:S(2)}) copy-start(f32[4,8,1,384]{3,1,2,0:T(8,128)S(1)} %copy.2603) | copy-start | bytes 147460
  16.0 8.0 %copy-start.36 = (f32[4,8,1,384]{3,1,2,0:T(8,128)}, f32[4,8,1,384]{3,1,2,0:T(8,128)S(1)}, u32[]{:S(2)}) copy-start(f32[4,8,1,384]{3,1,2,0:T(8,128)S(1)} %copy.2604) | copy-start | bytes 147460
  16.0 8.0 %copy-start.37 = (f32[4,8,1,384]{3,1,2,0:T(8,128)}, f32[4,8,1,384]{3,1,2,0:T(8,128)S(1)}, u32[]{:S(2)}) copy-start(f32[4,8,1,384]{3,1,2,0:T(8,128)S(1)} %copy.2605) | copy-start | bytes 147460
  16.1 8.0 %copy-start.38 = (f32[4,8,1,384]{3,1,2,0:T(8,128)}, f32[4,8,1,384]{3,1,2,0:T(8,128)S(1)}, u32[]{:S(2)}) copy-start(f32[4,8,1,384]{3,1,2,0:T(8,128)S(1)} %copy.2606) | copy-start | bytes 147460
  16.1 8.0 %copy-start.39 = (f32[4,8,1,384]{3,1,2,0:T(8,128)}, f32[4,8,1,384]{3,1,2,0:T(8,128)S(1)}, u32[]{:S(2)}) copy-start(f32[4,8,1,384]{3,1,2,0:T(8,128)S(1)} %copy.2607) | copy-start | bytes 147460
  16.1 8.0 %copy-start.40 = (f32[4,8,1,384]{3,1,2,0:T(8,128)}, f32[4,8,1,384]{3,1,2,0:T(8,128)S(1)}, u32[]{:S(2)}) copy-start(f32[4,8,1,384]{3,1,2,0:T(8,128)S(1)} %copy.2608) | copy-start | bytes 147460
  16.4 7.7 %copy-start.41 = (f32[4,8,1,384]{3,1,2,0:T(8,128)}, f32[4,8,1,384]{3,1,2,0:T(8,128)S(1)}, u32[]{:S(2)}) copy-start(f32[4,8,1,384]{3,1,2,0:T(8,128)S(1)} %copy.2601) | copy-start | bytes 147460
  16.4 7.7 %copy-start.42 = (f32[4,8,1,384]{3,1,2,0:T(8,128)}, f32[4,8,1,384]{3,1,2,0:T(8,128)S(1)}, u32[]{:S(2)}) copy-start(f32[4,8,1,384]{3,1,2,0:T(8,128)S(1)} %copy.2594) | copy-start | bytes 147460
  16.4 7.7 %copy-start.43 = (f32[4,8,1,384]{3,1,2,0:T(8,128)}, f32[4,8,1,384]{3,1,2,0:T(8,128)S(1)}, u32[]{:S(2)}) copy-start(f32[4,8,1,384]{3,1,2,0:T(8,128)S(1)} %copy.2595) | copy-start | bytes 147460
  16.5 7.6 %copy-start.44 = (f32[4,8,1,384]{3,1,2,0:T(8,128)}, f32[4,8,1,384]{3,1,2,0:T(8,128)S(1)}, u32[]{:S(2)}) copy-start(f32[4,8,1,384]{3,1,2,0:T(8,128)S(1)} %copy.2596) | copy-start | bytes 147460
  16.5 7.6 %copy-start.45 = (f32[4,8,1,384]{3,1,2,0:T(8,128)}, f32[4,8,1,384]{3,1,2,0:T(8,128)S(1)}, u32[]{:S(2)}) copy-start(f32[4,8,1,384]{3,1,2,0:T(8,128)S(1)} %copy.2597) | copy-start | bytes 147460
  16.5 7.6 %copy-start.46 = (f32[4,8,1,384]{3,1,2,0:T(8,128)}, f32[4,8,1,384]{3,1,2,0:T(8,128)S(1)}, u32[]{:S(2)}) copy-start(f32[4,8,1,384]{3,1,2,0:T(8,128)S(1)} %copy.2598) | copy-start | bytes 147460
  16.5 7.6 %copy-start.47 = (f32[4,8,1,384]{3,1,2,0:T(8,128)}, f32[4,8,1,384]{3,1,2,0:T(8,128)S(1)}, u32[]{:S(2)}) copy-start(f32[4,8,1,384]{3,1,2,0:T(8,128)S(1)} %copy.2599) | copy-start | bytes 147460
  16.6 7.6 %copy-start.48 = (f32[4,8,1,384]{3,1,2,0:T(8,128)}, f32[4,8,1,384]{3,1,2,0:T(8,128)S(1)}, u32[]{:S(2)}) copy-start(f32[4,8,1,384]{3,1,2,0:T(8,128)S(1)} %copy.2600) | copy-start | bytes 147460
  16.6 2.4 copy-start.62
  16.6 2.4 copy-start.63
  16.6 2.4 copy-start.71
  16.9 5.0 %copy-start.17 = (f32[4,8,1,384]{3,1,2,0:T(8,128)}, f32[4,8,1,384]{3,1,2,0:T(8,128)S(1)}, u32[]{:S(2)}) copy-start(f32[4,8,1,384]{3,1,2,0:T(8,128)S(1)} %copy.2611) | copy-start | bytes 147460
  17.0 5.0 %copy-start.18 = (f32[4,8,1,384]{3,1,2,0:T(8,128)}, f32[4,8,1,384]{3,1,2,0:T(8,128)S(1)}, u32[]{:S(2)}) copy-start(f32[4,8,1,384]{3,1,2,0:T(8,128)S(1)} %copy.2612) | copy-start | bytes 147460
  17.0 5.0 %copy-start.19 = (f32[4,8,1,384]{3,1,2,0:T(8,128)}, f32[4,8,1,384]{3,1,2,0:T(8,128)S(1)}, u32[]{:S(2)}) copy-start(f32[4,8,1,384]{3,1,2,0:T(8,128)S(1)} %copy.2613) | copy-start | bytes 147460
  17.0 5.0 %copy-start.20 = (f32[4,8,1,384]{3,1,2,0:T(8,128)}, f32[4,8,1,384]{3,1,2,0:T(8,128)S(1)}, u32[]{:S(2)}) copy-start(f32[4,8,1,384]{3,1,2,0:T(8,128)S(1)} %copy.2614) | copy-start | bytes 147460
  17.0 4.9 %copy-start.21 = (f32[4,8,1,384]{3,1,2,0:T(8,128)}, f32[4,8,1,384]{3,1,2,0:T(8,128)S(1)}, u32[]{:S(2)}) copy-start(f32[4,8,1,384]{3,1,2,0:T(8,128)S(1)} %copy.2615) | copy-start | bytes 147460
  17.1 4.9 %copy-start.22 = (f32[4,8,1,384]{3,1,2,0:T(8,128)}, f32[4,8,1,384]{3,1,2,0:T(8,128)S(1)}, u32[]{:S(2)}) copy-start(f32[4,8,1,384]{3,1,2,0:T(8,128)S(1)} %copy.2616) | copy-start | bytes 147460
  17.3 4.6 %copy-start.23 = (f32[4,8,1,384]{3,1,2,0:T(8,128)}, f32[4,8,1,384]{3,1,2,0:T(8,128)S(1)}, u32[]{:S(2)}) copy-start(f32[4,8,1,384]{3,1,2,0:T(8,128)S(1)} %copy.2625) | copy-start | bytes 147460
  17.4 4.6 %copy-start.24 = (f32[4,8,1,384]{3,1,2,0:T(8,128)}, f32[4,8,1,384]{3,1,2,0:T(8,128)S(1)}, u32[]{:S(2)}) copy-start(f32[4,8,1,384]{3,1,2,0:T(8,128)S(1)} %copy.2618) | copy-start | bytes 147460
  17.4 4.6 %copy-start.25 = (f32[4,8,1,384]{3,1,2,0:T(8,128)}, f32[4,8,1,384]{3,1,2,0:T(8,128)S(1)}, u32[]{:S(2)}) copy-start(f32[4,8,1,384]{3,1,2,0:T(8,128)S(1)} %copy.2619) | copy-start | bytes 147460
  17.4 4.6 %copy-start.26 = (f32[4,8,1,384]{3,1,2,0:T(8,128)}, f32[4,8,1,384]{3,1,2,0:T(8,128)S(1)}, u32[]{:S(2)}) copy-start(f32[4,8,1,384]{3,1,2,0:T(8,128)S(1)} %copy.2620) | copy-start | bytes 147460
  17.4 4.6 %copy-start.27 = (f32[4,8,1,384]{3,1,2,0:T(8,128)}, f32[4,8,1,384]{3,1,2,0:T(8,128)S(1)}, u32[]{:S(2)}) copy-start(f32[4,8,1,384]{3,1,2,0:T(8,128)S(1)} %copy.2621) | copy-start | bytes 147460
  17.5 4.6 %copy-start.28 = (f32[4,8,1,384]{3,1,2,0:T(8,128)}, f32[4,8,1,384]{3,1,2,0:T(8,128)S(1)}, u32[]{:S(2)}) copy-start(f32[4,8,1,384]{3,1,2,0:T(8,128)S(1)} %copy.2622) | copy-start | bytes 147460
  17.5 4.6 %copy-start.29 = (f32[4,8,1,384]{3,1,2,0:T(8,128)}, f32[4,8,1,384]{3,1,2,0:T(8,128)S(1)}, u32[]{:S(2)}) copy-start(f32[4,8,1,384]{3,1,2,0:T(8,128)S(1)} %copy.2623) | copy-start | bytes 147460
  17.5 4.6 %copy-start.30 = (f32[4,8,1,384]{3,1,2,0:T(8,128)}, f32[4,8,1,384]{3,1,2,0:T(8,128)S(1)}, u32[]{:S(2)}) copy-start(f32[4,8,1,384]{3,1,2,0:T(8,128)S(1)} %copy.2624) | copy-start | bytes 147460
  20.8 4.4 %copy-start.1 = (bf16[2,1,5,384,384]{4,3,2,1,0:T(8,128)(2,1)S(1)}, bf16[2,1,5,384,384]{4,3,2,1,0:T(8,128)(2,1)}, u32[]{:S(2)}) copy-start(bf16[2,1,5,384,384]{4,3,2,1,0:T(8,128)(2,1)} %param.26) | copy-start | bytes 8847364
  20.8 4.3 %copy-start.13 = (bf16[4,8,19,384]{3,1,2,0:T(8,128)(2,1)S(1)}, bf16[4,8,19,384]{3,1,2,0:T(8,128)(2,1)}, u32[]{:S(2)}) copy-start(bf16[4,8,19,384]{3,1,2,0:T(8,128)(2,1)} %param.25) | copy-start | bytes 1400836
  27.3 54.6 %collective-permute-start = (bf16[4,19,8,384]{3,2,1,0:T(8,128)(2,1)S(1)}, bf16[4,19,8,384]{3,2,1,0:T(8,128)(2,1)}, u32[]{:S(2)}, u32[]{:S(2)}) collective-permute-start(bf16[4,19,8,384]{3,2,1,0:T(8,128)(2,1)S(1)} %get-tuple-element.170), channel_id=1, source_target_pairs={{0,96},{32,0},{64,32},{96,64},{1,97},{33,1},{65,33},{97,65},{2,98}... | collective-permute-start | bytes 1400840 | tf_op jit(solution)/shard_map/ppermute | solution.py:140
  53.1 18.9 %copy-start.58 = (bf16[384,384]{1,0:T(8,128)(2,1)S(1)}, bf16[384,384]{1,0:T(8,128)(2,1)}, u32[]{:S(2)}) copy-start(bf16[384,384]{1,0:T(8,128)(2,1)} %get-tuple-element.1638) | copy-start | bytes 884740
  53.1 18.9 %copy-start.59 = (bf16[384,384]{1,0:T(8,128)(2,1)S(1)}, bf16[384,384]{1,0:T(8,128)(2,1)}, u32[]{:S(2)}) copy-start(bf16[384,384]{1,0:T(8,128)(2,1)} %get-tuple-element.1639) | copy-start | bytes 884740
  53.1 18.9 %copy-start.66 = (bf16[4,32,384]{2,1,0:T(8,128)(2,1)S(1)}, bf16[4,32,384]{2,1,0:T(8,128)(2,1)}, u32[]{:S(2)}) copy-start(bf16[4,32,384]{2,1,0:T(8,128)(2,1)} %fusion.310) | copy-start | bytes 294916
  53.1 18.9 %copy-start.69 = (bf16[4,32,384]{2,1,0:T(8,128)(2,1)S(1)}, bf16[4,32,384]{2,1,0:T(8,128)(2,1)}, u32[]{:S(2)}) copy-start(bf16[4,32,384]{2,1,0:T(8,128)(2,1)} %get-tuple-element.1731) | copy-start | bytes 294916
  53.1 18.9 %copy-start.70 = (bf16[4,32,384]{2,1,0:T(8,128)(2,1)S(1)}, bf16[4,32,384]{2,1,0:T(8,128)(2,1)}, u32[]{:S(2)}) copy-start(bf16[4,32,384]{2,1,0:T(8,128)(2,1)} %get-tuple-element.1732) | copy-start | bytes 294916
  62.2 19.7 %copy-start.2 = (bf16[2,1,5,384,384]{4,3,2,1,0:T(8,128)(2,1)S(1)}, bf16[2,1,5,384,384]{4,3,2,1,0:T(8,128)(2,1)}, u32[]{:S(2)}) copy-start(bf16[2,1,5,384,384]{4,3,2,1,0:T(8,128)(2,1)} %param.26) | copy-start | bytes 8847364
  83.9 11.5 %collective-permute-start.1 = (bf16[4,19,8,384]{3,2,1,0:T(8,128)(2,1)}, bf16[4,19,8,384]{3,2,1,0:T(8,128)(2,1)S(1)}, u32[]{:S(2)}, u32[]{:S(2)}) collective-permute-start(bf16[4,19,8,384]{3,2,1,0:T(8,128)(2,1)} %get-tuple-element.171), channel_id=1, source_target_pairs={{0,96},{32,0},{64,32},{96,64},{1,97},{33,1},{65,33},{97,65},{2,98}... | collective-permute-start | bytes 1400840 | tf_op jit(solution)/shard_map/ppermute | solution.py:140
  87.5 8.0 %copy-start.10 = (f32[4,19,8,384]{3,2,1,0:T(8,128)}, f32[4,19,8,384]{3,2,1,0:T(8,128)S(1)}, u32[]{:S(2)}) copy-start(f32[4,19,8,384]{3,2,1,0:T(8,128)S(1)} %add_dynamic-update-slice_fusion) | copy-start | bytes 2801668
  98.0 25.8 %collective-permute-start.2 = (bf16[4,19,8,384]{3,2,1,0:T(8,128)(2,1)}, bf16[4,19,8,384]{3,2,1,0:T(8,128)(2,1)S(1)}, u32[]{:S(2)}, u32[]{:S(2)}) collective-permute-start(bf16[4,19,8,384]{3,2,1,0:T(8,128)(2,1)} %copy-done.15), channel_id=1, source_target_pairs={{0,96},{32,0},{64,32},{96,64},{1,97},{33,1},{65,33},{97,65},{2,98}... | collective-permute-start | bytes 1400840 | tf_op jit(solution)/shard_map/ppermute | solution.py:140
  123.8 19.4 %copy-start.32 = (f32[4,8,1,384]{3,1,2,0:T(8,128)S(1)}, f32[4,8,1,384]{3,1,2,0:T(8,128)}, u32[]{:S(2)}) copy-start(f32[4,8,1,384]{3,1,2,0:T(8,128)} %copy-done.31) | copy-start | bytes 147460
  123.8 19.4 %copy-start.34 = (f32[4,8,1,384]{3,1,2,0:T(8,128)S(1)}, f32[4,8,1,384]{3,1,2,0:T(8,128)}, u32[]{:S(2)}) copy-start(f32[4,8,1,384]{3,1,2,0:T(8,128)} %copy-done.33) | copy-start | bytes 147460
  123.8 19.4 %copy-start.64 = (f32[4,3,1,384]{3,1,0,2:T(4,128)S(1)}, f32[4,3,1,384]{3,1,0,2:T(4,128)}, u32[]{:S(2)}) copy-start(f32[4,3,1,384]{3,1,0,2:T(4,128)} %copy.2649) | copy-start | bytes 55300
  142.4 10.4 %collective-permute-start.3 = (bf16[4,19,8,384]{3,2,1,0:T(8,128)(2,1)}, bf16[4,19,8,384]{3,2,1,0:T(8,128)(2,1)S(1)}, u32[]{:S(2)}, u32[]{:S(2)}) collective-permute-start(bf16[4,19,8,384]{3,2,1,0:T(8,128)(2,1)} %copy-done.14), channel_id=1, source_target_pairs={{0,96},{32,0},{64,32},{96,64},{1,97},{33,1},{65,33},{97,65},{2,98}... | collective-permute-start | bytes 1400840 | tf_op jit(solution)/shard_map/ppermute | solution.py:140
  154.6 24.6 %collective-permute-start.4 = (bf16[4,19,8,384]{3,2,1,0:T(8,128)(2,1)S(1)}, bf16[4,19,8,384]{3,2,1,0:T(8,128)(2,1)}, u32[]{:S(2)}, u32[]{:S(2)}) collective-permute-start(bf16[4,19,8,384]{3,2,1,0:T(8,128)(2,1)S(1)} %get-tuple-element.174), channel_id=1, source_target_pairs={{0,96},{32,0},{64,32},{96,64},{1,97},{33,1},{65,33},{97,65},{2,98}... | collective-permute-start | bytes 1400840 | tf_op jit(solution)/shard_map/ppermute | solution.py:140
  179.2 5.4 %copy-start.77 = (s32[4]{0:T(128)S(1)}, s32[4]{0:T(128)}, u32[]{:S(2)}) copy-start(s32[4]{0:T(128)} %param.31) | copy-start | bytes 52
  181.1 10.3 %collective-permute-start.5 = (bf16[4,19,8,384]{3,2,1,0:T(8,128)(2,1)}, bf16[4,19,8,384]{3,2,1,0:T(8,128)(2,1)S(1)}, u32[]{:S(2)}, u32[]{:S(2)}) collective-permute-start(bf16[4,19,8,384]{3,2,1,0:T(8,128)(2,1)} %get-tuple-element.175), channel_id=1, source_target_pairs={{0,96},{32,0},{64,32},{96,64},{1,97},{33,1},{65,33},{97,65},{2,98}... | collective-permute-start | bytes 1400840 | tf_op jit(solution)/shard_map/ppermute | solution.py:140
  193.9 40.1 %collective-permute-start.6 = (bf16[4,19,8,384]{3,2,1,0:T(8,128)(2,1)}, bf16[4,19,8,384]{3,2,1,0:T(8,128)(2,1)S(1)}, u32[]{:S(2)}, u32[]{:S(2)}) collective-permute-start(bf16[4,19,8,384]{3,2,1,0:T(8,128)(2,1)} %copy-done.16), channel_id=1, source_target_pairs={{0,96},{32,0},{64,32},{96,64},{1,97},{33,1},{65,33},{97,65},{2,98}... | collective-permute-start | bytes 1400840 | tf_op jit(solution)/shard_map/ppermute | solution.py:140
  210.9 23.1 %copy-start.3 = (bf16[2,1,5,384,384]{4,3,2,1,0:T(8,128)(2,1)S(1)}, bf16[2,1,5,384,384]{4,3,2,1,0:T(8,128)(2,1)}, u32[]{:S(2)}) copy-start(bf16[2,1,5,384,384]{4,3,2,1,0:T(8,128)(2,1)} %param.26) | copy-start | bytes 8847364
  210.9 23.1 %copy-start.11 = (f32[4,19,8,384]{3,2,1,0:T(8,128)S(1)}, f32[4,19,8,384]{3,2,1,0:T(8,128)}, u32[]{:S(2)}) copy-start(f32[4,19,8,384]{3,2,1,0:T(8,128)} %subtract_dynamic-update-slice_fusion.2) | copy-start | bytes 2801668
  250.3 164.3 %all-reduce.7.cloned.1.call-start = ((), (), s32[]{:S(2)}) async-start(), calls=%async_computation.1 | async-start | bytes 11796480
  250.6 3.6 copy-start.12
  (21 other events, 31.8 us)
Sparse Core Ops, SparseCore 0:
  250.4 43.6 all-reduce.4
  297.9 116.6 all-reduce.6
where the time goes:
time: 430 us; the launch traced here: 424 us
  waiting for transfers between devices  216 us (50%)
  local copies, waits for them, and re-layouts  84.6 us (20%)
  starting transfers between devices  59 us (14%)
  other arithmetic  33.8 us (8%)
  between operations  17.5 us (4%)
  matrix products  11.2 us (3%)
    unnamed x4, waiting for transfers between devices  148 us
    ppermute x7, waiting for transfers between devices, body(): g = lax.ppermute(g, 'section', perm)  67.4 us
    ppermute x7, starting transfers between devices, body(): g = lax.ppermute(g, 'section', perm)  58.6 us
    unnamed x230, local copies, waits for them, and re-layouts  16.8 us
    mul x102, local copies, waits for them, and re-layouts, apply(): total = total + tab[:, None] * v[:, :, n:n + 1]  15.9 us
    unnamed x9, other arithmetic  11.9 us
    another operation x6, local copies, waits for them, and re-layouts  10.8 us
    cond x2, local copies, waits for them, and re-layouts, body(): lax.cond(active, lambda v: backward(lap, v), lambda v: (v, jnp.zeros((5,...  9.59 us
  transfers between devices with their start and end apart: 9, of which 8 were waited for; matrix products, arithmetic and copies ran while one was open for 15% of the time, Pallas kernels for 0%

commit v1 on v0

v1 whole, which is shorter than its diff:
```python
import functools
import math

import jax
import jax.numpy as jnp
from jax import lax
from jax.experimental import pallas as pl
from jax.experimental.pallas import tpu as pltpu
from jax.sharding import PartitionSpec as P

F32 = jnp.float32
BF16 = jnp.bfloat16
MESH = pl.DeviceIdType.MESH
LANES = 128
ROWS = 160
BLOCKS = ROWS // 8


def dot(a, b):
    return jnp.dot(a, b, preferred_element_type=F32)


def dot_nt(a, b):
    return lax.dot_general(a, b, (((1,), (1,)), ((), ())), preferred_element_type=F32)


def dot_tn(a, b):
    return lax.dot_general(a, b, (((0,), (0,)), ((), ())), preferred_element_type=F32)


def mix_atoms(table, values, lanes, back):
    flat = None
    pairs = []
    for n in range(8):
        term = table(0, n)[None] * values(1, 6, n)
        flat = term if flat is None else flat + term
    for lo, mid, hi, t in ((6, 10, 14, 1), (14, 17, 20, 3)):
        plus = minus = None
        for n in range(8):
            c, q = table(t, n)[None], table(t + 1, n)[None]
            p, m = values(lo, mid, n), values(mid, hi, n)
            if back:
                up, um = c * p - q * m, q * p + c * m
            else:
                up, um = c * p + q * m, c * m - q * p
            plus = up if plus is None else plus + up
            minus = um if minus is None else minus + um
        pairs += [plus, minus]
    return flat, pairs


def kernel(
    n_dp, scale, h, g0, w, radial, angle, atoms, ecount, acount, in_grad, wout,
    trig, tab_f, tab_b, hx, hs, x1, x2, y, summed, gates, dref, ub0, ub1, ub2,
    rbuf, obuf, fb, frx, dwf, pf, pk, prx, st, rs,
    ring_send, ring_recv, fin_send, fin_recv, pair_send, pair_recv, plane_send, plane_recv,
):
    batches, atom_slots, coeff_rows, channels = g0.shape
    edges = angle.shape[1]
    section = lax.axis_index("section")
    dp = lax.axis_index("dp")
    core = lax.rem(dp, 2)
    chip = dp // 2
    chips = n_dp // 2
    share = channels // n_dp
    packed = pk.shape[3]
    tiles = [pl.ds(LANES * j, LANES) for j in range(channels // LANES)]

    barrier = pltpu.get_barrier_semaphore()
    for off in range(1, 4):
        pl.semaphore_signal(barrier, inc=1, device_id=(lax.rem(section + off, 4), dp), device_id_type=MESH)
    pl.semaphore_signal(barrier, inc=1, device_id=(section, dp + 1 - 2 * core), device_id_type=MESH)

    def greet(off, carry):
        peer = lax.rem(chip + off, chips) * 2 + core
        pl.semaphore_signal(barrier, inc=1, device_id=(section, peer), device_id_type=MESH)
        return carry

    lax.fori_loop(1, chips, greet, 0)

    turn = jnp.concatenate([angle[...], 2.0 * angle[...]], 0)
    trig[0] = jnp.cos(turn)
    trig[1] = jnp.sin(turn)

    def make_tables(b, carry):
        dst = atoms[b, 0:1, :]
        src = atoms[b, 1:2, :]
        edge = lax.broadcasted_iota(jnp.int32, (1, edges), 1)
        live = jnp.where(edge < ecount[b], 0.25, 0.0).astype(F32)
        factors = [live]
        for m in range(2):
            for f in range(2):
                factors.append(live * trig[f, pl.ds(batches * m + b, 1), :])
        slot = lax.broadcasted_iota(jnp.int32, (64, edges), 0)
        for code, tab in ((src * 8 + dst, tab_f), (dst * 8 + src, tab_b)):
            hit = slot == code
            pick = jnp.concatenate([jnp.where(hit, f, 0.0) for f in factors], 0)
            high = pick.astype(BF16)
            low = (pick - high.astype(F32)).astype(BF16)
            rad = radial[b]
            tab[b] = (dot(high, rad) + dot(low, rad)).reshape(5, 8, 8, channels)
        return carry

    lax.fori_loop(0, batches, make_tables, 0)

    hx[:, 0:8, :] = jnp.zeros((len(tiles), 8, LANES), F32)

    def turn_in(read):
        for a in range(atom_slots):
            v = read(a).astype(F32)
            for j in range(len(tiles)):
                hx[j, pl.ds(8 + a, coeff_rows, stride=8), :] = v[:, LANES * j : LANES * (j + 1)]
        return jnp.concatenate([hx[j] for j in range(len(tiles))], 1)

    def forward(lap):
        def gather(b, carry):
            v = turn_in(lambda a: h[lap, b, a])
            hs[lap, b] = v.astype(BF16)
            for ref, lo, mid, hi in ((x1, 48, 80, 112), (x2, 112, 136, 160)):
                p, m = v[lo:mid], v[mid:hi]
                ref[b, :, 0:channels] = jnp.concatenate([p, m], 0).astype(BF16)
                ref[b, :, channels:] = jnp.concatenate([-m, p], 0).astype(BF16)
            return carry

        lax.fori_loop(0, batches, gather, 0)
        x0 = hs[lap, :, 0:48, :].reshape(batches * 48, channels)
        y[:, 0:6] = dot(x0, w[lap, 0]).reshape(batches, 6, 8, channels)
        w1 = w[lap, 1:3].reshape(2 * channels, channels)
        y[:, 6:14] = dot(x1[...].reshape(batches * 64, 2 * channels), w1).reshape(batches, 8, 8, channels)
        w2 = w[lap, 3:5].reshape(2 * channels, channels)
        y[:, 14:20] = dot(x2[...].reshape(batches * 48, 2 * channels), w2).reshape(batches, 6, 8, channels)

        def collect(b, carry):
            for lanes in tiles:
                flat, pairs = mix_atoms(
                    lambda t, n: tab_f[b, t, n, :, lanes],
                    lambda lo, hi, n: y[b, lo:hi, n : n + 1, lanes],
                    lanes,
                    False,
                )
                summed[lap, b, 1:6, :, lanes] = flat
                summed[lap, b, 6:10, :, lanes] = pairs[0]
                summed[lap, b, 10:14, :, lanes] = pairs[1]
                summed[lap, b, 14:17, :, lanes] = pairs[2]
                summed[lap, b, 17:20, :, lanes] = pairs[3]
                gates[lap, b, :, lanes] = jax.nn.sigmoid(flat[0])
            return carry

        lax.fori_loop(0, batches, collect, 0)

    def ring_copy(lap, b):
        there = jnp.where(section == 0, 0, lap)
        slot_there = there * batches + b
        return pltpu.make_async_remote_copy(
            src_ref=obuf.at[lap * batches + b],
            dst_ref=rbuf.at[slot_there],
            send_sem=ring_send.at[lap * batches + b],
            recv_sem=ring_recv.at[slot_there],
            device_id=(lax.rem(section + 3, 4), dp),
            device_id_type=MESH,
        )

    def ring_arrival(lap, b):
        slot = lap * batches + b
        return pltpu.make_async_remote_copy(
            src_ref=obuf.at[slot],
            dst_ref=rbuf.at[slot],
            send_sem=ring_send.at[slot],
            recv_sem=ring_recv.at[slot],
            device_id=(lax.rem(section + 3, 4), dp),
            device_id_type=MESH,
        )

    def final_copy(b, to):
        return pltpu.make_async_remote_copy(
            src_ref=fb.at[b, to],
            dst_ref=frx.at[b],
            send_sem=fin_send.at[b, to],
            recv_sem=fin_recv.at[b],
            device_id=(to, dp),
            device_id_type=MESH,
        )

    def backward(lap, b):
        slot = lap * batches + b

        @pl.when((section == 3) & (lap == 1))
        def _():
            rbuf[slot] = turn_in(lambda a: g0[b, a]).astype(BF16)

        @pl.when((section != 3) | (lap == 0))
        def _():
            ring_arrival(lap, b).wait_recv()

        for lanes in tiles:
            g = rbuf[slot, :, lanes].astype(F32).reshape(BLOCKS, 8, LANES)
            gate = gates[lap, b, :, lanes]
            extra = jnp.sum(g[1:] * summed[lap, b, 1:, :, lanes], 0) * gate * (1.0 - gate)
            d = g * gate[None]
            dref[:, :, lanes] = d
            dref[1, :, lanes] = d[1] + extra
        for j, lanes in enumerate(tiles):
            flat, pairs = mix_atoms(
                lambda t, n: tab_b[b, t, n, :, lanes],
                lambda lo, hi, n: dref[lo:hi, n : n + 1, lanes],
                lanes,
                True,
            )
            later = pl.ds(channels + LANES * j, LANES)
            pad = jnp.zeros((8, LANES), F32)
            ub0[lap, b, :, lanes] = jnp.concatenate([pad, flat.reshape(40, LANES)], 0).astype(BF16)
            for ref, (up, um) in ((ub1, pairs[0:2]), (ub2, pairs[2:4])):
                up = up.reshape(-1, LANES)
                um = um.reshape(-1, LANES)
                ref[lap, b, :, lanes] = jnp.concatenate([up, um], 0).astype(BF16)
                ref[lap, b, :, later] = jnp.concatenate([um, -up], 0).astype(BF16)
        w1 = jnp.concatenate([w[lap, 1], w[lap, 2]], 1)
        out = rbuf[slot, 48:112, :].astype(F32) + dot_nt(ub1[lap, b], w1)
        obuf[slot, 48:112, :] = out.astype(BF16)
        w2 = jnp.concatenate([w[lap, 3], w[lap, 4]], 1)
        out = rbuf[slot, 112:160, :].astype(F32) + dot_nt(ub2[lap, b], w2)
        obuf[slot, 112:160, :] = out.astype(BF16)
        out = rbuf[slot, 0:48, :].astype(F32) + dot_nt(ub0[lap, b], w[lap, 0])
        obuf[slot, 0:48, :] = out.astype(BF16)

        @pl.when((section != 0) | (lap == 1))
        def _():
            ring_copy(lap, b).start()

        @pl.when((section == 0) & (lap == 0))
        def _():
            for j, lanes in enumerate(tiles):
                hx[j] = obuf[slot, :, lanes].astype(F32)
            for to in range(4):
                for n in range(2):
                    atom = 2 * to + n
                    keep = jnp.where(acount[b] > atom, 1.0, 0.0).astype(F32)
                    for j, lanes in enumerate(tiles):
                        part = hx[j, pl.ds(8 + atom, coeff_rows, stride=8), :] * keep
                        fb[b, to, n, 0:coeff_rows, lanes] = part.astype(BF16)
            for to in range(1, 4):
                final_copy(b, to).start()

    def pair_copy(lap):
        return pltpu.make_async_remote_copy(
            src_ref=pk.at[lap, 1 - core],
            dst_ref=prx.at[lap],
            send_sem=pair_send.at[lap],
            recv_sem=pair_recv.at[lap],
            device_id=(section, dp + 1 - 2 * core),
            device_id_type=MESH,
        )

    def weight_term(lap):
        h0 = hs[lap, :, 0:48, :].reshape(batches * 48, channels)
        dwf[0] = dot_tn(h0, ub0[lap].reshape(batches * 48, channels))
        h1 = hs[lap, :, 48:112, :].reshape(batches * 64, channels)
        both = dot_tn(h1, ub1[lap].reshape(batches * 64, 2 * channels))
        dwf[1] = both[:, :channels]
        dwf[2] = both[:, channels:]
        h2 = hs[lap, :, 112:160, :].reshape(batches * 48, channels)
        both = dot_tn(h2, ub2[lap].reshape(batches * 48, 2 * channels))
        dwf[3] = both[:, :channels]
        dwf[4] = both[:, channels:]

        def pack(j, carry):
            for k in range(5):
                rows = dwf[k, pl.ds(pl.multiple_of(2 * share * j, 8), 2 * share), :]
                pf[0, share * k : share * (k + 1), :] = rows[:share]
                pf[1, share * k : share * (k + 1), :] = rows[share:]
            pk[lap, 0, j] = pf[0].astype(BF16)
            pk[lap, 1, j] = pf[1].astype(BF16)
            return carry

        lax.fori_loop(0, chips, pack, 0)
        pair_copy(lap).start()

    def plane_copy(lap, to):
        return pltpu.make_async_remote_copy(
            src_ref=st.at[lap, to],
            dst_ref=rs.at[lap, chip],
            send_sem=plane_send.at[lap, to],
            recv_sem=plane_recv.at[lap, chip],
            device_id=(section, to * 2 + core),
            device_id_type=MESH,
        )

    def plane_arrival(lap, source):
        return pltpu.make_async_remote_copy(
            src_ref=st.at[lap, source],
            dst_ref=rs.at[lap, source],
            send_sem=plane_send.at[lap, source],
            recv_sem=plane_recv.at[lap, source],
            device_id=(section, source * 2 + core),
            device_id_type=MESH,
        )

    def spread(lap):
        pair_copy(lap).wait_recv()

        def add(off, carry):
            j = lax.rem(chip + off, chips)
            st[lap, j] = (pk[lap, core, j].astype(F32) + prx[lap, j].astype(F32)).astype(BF16)

            @pl.when(off < chips)
            def _():
                plane_copy(lap, j).start()

            return carry

        lax.fori_loop(1, chips + 1, add, 0)

    def gather_grads(lap):
        wout[lap] = st[lap, chip].astype(F32)

        def take(off, carry):
            j = lax.rem(chip + off, chips)
            plane_arrival(lap, j).wait_recv()
            wout[lap] += rs[lap, j].astype(F32)
            return carry

        lax.fori_loop(1, chips, take, 0)
        wout[lap] = wout[lap] * scale

    pf[...] = jnp.zeros_like(pf)

    @pl.when(section == 0)
    def _():
        fb[...] = jnp.zeros_like(fb)

    forward(1)
    pl.semaphore_wait(barrier, 4 + chips - 1)

    def step(i, carry):
        lap = 1 - i // batches
        b = lax.rem(i, batches)

        @pl.when(((i == 0) & (section != 3)) | ((i == batches) & (section == 3)))
        def _():
            forward(0)

        @pl.when(i == batches)
        def _():
            weight_term(1)

        backward(lap, b)

        @pl.when(i == batches)
        def _():
            spread(1)

        return carry

    lax.fori_loop(0, 2 * batches, step, 0)
    weight_term(0)
    spread(0)
    gather_grads(1)

    @pl.when(section == 0)
    def _():
        for b in range(batches):
            in_grad[b] = fb[b, 0]
            for to in range(1, 4):
                final_copy(b, to).wait_send()

    @pl.when(section != 0)
    def _():
        for b in range(batches):
            final_copy(b, section).wait_recv()
            in_grad[b] = frx[b]

    gather_grads(0)

    def ring_left(i, carry):
        lap = 1 - i // batches

        @pl.when((section != 0) | (lap == 1))
        def _():
            ring_copy(lap, lax.rem(i, batches)).wait_send()

        return carry

    lax.fori_loop(0, 2 * batches, ring_left, 0)
    for lap in (1, 0):
        pair_copy(lap).wait_send()

        def left(off, carry):
            plane_copy(lap, lax.rem(chip + off, chips)).wait_send()
            return carry

        lax.fori_loop(1, chips, left, 0)


def body(n_dp, h_saved, out_cot, so2_weight, radial, edge_angle, edge_atoms, edge_count, atom_count):
    batches, atom_slots, coeff_rows, channels = out_cot.shape
    edges = edge_angle.shape[1]
    share = channels // n_dp
    packed = -(-5 * share // 16) * 16
    chips = n_dp // 2
    slots = 2 * batches
    scale = 1.0 / math.sqrt(n_dp * batches * edges)
    vmem = pl.BlockSpec(memory_space=pltpu.VMEM)
    smem = pl.BlockSpec(memory_space=pltpu.SMEM)
    dma = pltpu.SemaphoreType.DMA
    in_grad, wout = pl.pallas_call(
        functools.partial(kernel, n_dp, scale),
        out_shape=(
            jax.ShapeDtypeStruct((batches, 2, 32, channels), BF16),
            jax.ShapeDtypeStruct((2, packed, channels), F32),
        ),
        in_specs=[vmem] * 6 + [smem] * 2,
        out_specs=(vmem, vmem),
        scratch_shapes=[
            pltpu.VMEM((2, 2 * batches, edges), F32),
            pltpu.VMEM((batches, 5, 8, 8, channels), F32),
            pltpu.VMEM((batches, 5, 8, 8, channels), F32),
            pltpu.VMEM((channels // LANES, ROWS, LANES), F32),
            pltpu.VMEM((2, batches, ROWS, channels), BF16),
            pltpu.VMEM((batches, 64, 2 * channels), BF16),
            pltpu.VMEM((batches, 48, 2 * channels), BF16),
            pltpu.VMEM((batches, BLOCKS, 8, channels), F32),
            pltpu.VMEM((2, batches, BLOCKS, 8, channels), F32),
            pltpu.VMEM((2, batches, 8, channels), F32),
            pltpu.VMEM((BLOCKS, 8, channels), F32),
            pltpu.VMEM((2, batches, 48, channels), BF16),
            pltpu.VMEM((2, batches, 64, 2 * channels), BF16),
            pltpu.VMEM((2, batches, 48, 2 * channels), BF16),
            pltpu.VMEM((slots, ROWS, channels), BF16),
            pltpu.VMEM((slots, ROWS, channels), BF16),
            pltpu.VMEM((batches, 4, 2, 32, channels), BF16),
            pltpu.VMEM((batches, 2, 32, channels), BF16),
            pltpu.VMEM((5, channels, channels), F32),
            pltpu.VMEM((2, packed, channels), F32),
            pltpu.VMEM((2, 2, chips, packed, channels), BF16),
            pltpu.VMEM((2, chips, packed, channels), BF16),
            pltpu.VMEM((2, chips, packed, channels), BF16),
            pltpu.VMEM((2, chips, packed, channels), BF16),
            dma((slots,)),
            dma((slots,)),
            dma((batches, 4)),
            dma((batches,)),
            dma((2,)),
            dma((2,)),
            dma((2, chips)),
            dma((2, chips)),
        ],
        compiler_params=pltpu.CompilerParams(
            collective_id=0, has_side_effects=True, vmem_limit_bytes=52 * 1024 * 1024
        ),
        name="window_backward",
    )(
        h_saved[:, 0], out_cot, so2_weight[:, 0], radial, edge_angle, edge_atoms, edge_count, atom_count
    )
    in_grad = in_grad[:, :, :coeff_rows]
    wout = wout[:, : 5 * share].reshape(2, 1, 5, share, channels)
    return in_grad, wout


def solution(mesh):
    placed = (
        P(None, "section", "dp", None, None, None),
        P("dp", None, None, None),
        P(None, "section", None, None, None),
        P("dp", None, None),
        P("dp", None),
        P("dp", None, None),
        P("dp"),
        P("dp"),
    )
    return jax.shard_map(
        functools.partial(body, mesh.shape["dp"]),
        mesh=mesh,
        in_specs=placed,
        out_specs=(P("dp", "section", None, None), P(None, "section", None, "dp", None)),
        check_vma=False,
    )
```

time: 430 us -> 75.9 us (0.18); the launches traced: 424 us -> 75.7 us
  waiting for transfers between devices: 216 us -> 0 us
  local copies, waits for them, and re-layouts: 84.6 us -> 5.34 us
  Pallas kernels: 0 us -> 69.6 us
  starting transfers between devices: 59 us -> 0 us
  other arithmetic: 33.8 us -> 0 us
  between operations: 17.5 us -> 0.72 us
  matrix products: 11.2 us -> 0 us
    unnamed x4 -> x0, waiting for transfers between devices: 148 us -> none
    pallas_call x0 -> x1, Pallas kernels: none -> 69.6 us  [body(): pl.pallas_call(functools.partial(kernel, n_dp, scale), out_shape=(jax.Sha...]
    ppermute x7 -> x0, waiting for transfers between devices: 67.4 us -> none  [body(): g = lax.ppermute(g, 'section', perm)]
    ppermute x7 -> x0, starting transfers between devices: 58.6 us -> none  [body(): g = lax.ppermute(g, 'section', perm)]
    mul x104 -> x0, local copies, waits for them, and re-layouts: 22.9 us -> none  [the longest x102 15.9 us: apply(): total = total + tab[:, None] * v[:, :, n:n + 1]]
    cond x32 -> x0, local copies, waits for them, and re-layouts: 16 us -> none  [the longest x2 9.59 us: body(): lax.cond(active, lambda v: backward(lap, v), lambda v: (v, jnp.zeros((5,...]
    another operation x8 -> x0, local copies, waits for them, and re-layouts: 12.5 us -> none
    unnamed x9 -> x0, other arithmetic: 11.9 us -> none
  transfers between devices with their start and end apart: 9 -> 0, of which waited for: 8 -> 0; matrix products, arithmetic and copies ran while one was open for 15% -> 0% of each run, Pallas kernels for 0% -> 0%
where the time goes in v1:
time: 75.9 us; the launch traced here: 75.7 us
  Pallas kernels  69.6 us (92%)
  local copies, waits for them, and re-layouts  5.34 us (7%)
    pallas_call x1, Pallas kernels, body(): pl.pallas_call(functools.partial(kernel, n_dp, scale), out_shape=(jax.Sha...  69.6 us
    unnamed x14, local copies, waits for them, and re-layouts  5.18 us

profile of v1, /device:TPU:1, one launch (start us, length us, event | category | flops | bytes accessed | tf_op | source)
XLA Modules:
  0.0 75.7 jit_solution(13908999490012853070)
XLA Ops:
  0.6 0.0 copy-start.4
  0.6 0.0 copy-start.3
  0.7 0.0 copy-start.1
  0.7 0.0 copy-start.2
  0.7 0.0 copy-start
  0.7 1.2 %copy.15.g0 = bf16[4,8,19,384]{3,2,1,0:T(8,128)(2,1)S(1)} copy(bf16[4,8,19,384]{3,1,2,0:T(8,128)(2,1)} %param.9) | data formatting | bytes 933888 | tf_op args[1]
  1.8 2.4 %copy.20 = bf16[2,1,4,8,19,384]{5,4,3,2,0,1:T(8,128)(2,1)} copy(bf16[2,1,4,8,19,384]{5,3,4,2,1,0:T(8,128)(2,1)} %param.8) | data formatting | bytes 1867776 | tf_op args[0]
  4.2 0.0 copy-done.4
  4.2 0.0 copy-done.3
  4.2 0.0 copy-done.1
  4.3 0.0 copy-done.2
  4.3 0.0 copy-done
  4.3 69.6 %window_backward.1 = (bf16[4,2,32,384]{3,2,1,0:T(8,128)(2,1)S(1)}, f32[2,64,384]{2,1,0:T(8,128)S(1)}) custom-call(bf16[2,4,8,19,384]{4,3,2,1,0:T(8,128)(2,1)} %bitcast.7, bf16[4,8,19,384]{3,2,1,0:T(8,128)(2,1)S(1)} %copy.15.g0, bf16[2,5,384,384]{3,2,1,0:T(8,128)(2,1)} %bitcast.8, bf16[4,112,384]{2,1,0:T(8,128)(2,1)S(1)} %copy-done, f32[4,112]{1,0:T(4,128)S(1)} %copy-done.2, ...), custom_call_target="tpu_custom_call" | custom-call | tf_op jit(solution)/shard_map/window_backward/pallas_call | solution.py:405
  74.0 0.7 copy.17
  74.7 0.1 copy.16
  74.8 0.9 %copy.18 = f32[2,1,5,12,384]{4,1,3,2,0:T(1,128)} copy(f32[2,1,5,12,384]{4,0,3,2,1:T(2,128)S(1)} %bitcast.9) | data formatting | bytes 368640
  (1 shorter events, 0.0 us)
Async XLA Ops:
  0.6 3.6 %copy-start.4 = (s32[4]{0:T(128)S(1)}, s32[4]{0:T(128)}, u32[]{:S(2)}) copy-start(s32[4]{0:T(128)} %acount.1) | copy-start | bytes 52
  0.6 3.6 %copy-start.3 = (s32[4]{0:T(128)S(1)}, s32[4]{0:T(128)}, u32[]{:S(2)}) copy-start(s32[4]{0:T(128)} %ecount.1) | copy-start | bytes 52
  0.7 3.6 %copy-start.1 = (s32[4,2,112]{2,1,0:T(2,128)S(1)}, s32[4,2,112]{2,1,0:T(2,128)}, u32[]{:S(2)}) copy-start(s32[4,2,112]{2,1,0:T(2,128)} %atoms.1) | copy-start | bytes 10756
  0.7 3.6 %copy-start.2 = (f32[4,112]{1,0:T(4,128)S(1)}, f32[4,112]{1,0:T(4,128)}, u32[]{:S(2)}) copy-start(f32[4,112]{1,0:T(4,128)} %angle.1) | copy-start | bytes 5380
  0.7 3.6 %copy-start = (bf16[4,112,384]{2,1,0:T(8,128)(2,1)S(1)}, bf16[4,112,384]{2,1,0:T(8,128)(2,1)}, u32[]{:S(2)}) copy-start(bf16[4,112,384]{2,1,0:T(8,128)(2,1)} %radial.1) | copy-start | bytes 1032196

commit v2 on v1

v2 whole, which is shorter than its diff:
```python
import functools
import math

import jax
import jax.numpy as jnp
from jax import lax
from jax.experimental import pallas as pl
from jax.experimental.pallas import tpu as pltpu
from jax.sharding import PartitionSpec as P

F32 = jnp.float32
BF16 = jnp.bfloat16
MESH = pl.DeviceIdType.MESH
LANES = 128
FIRST = (5, 13, 0)
COUNT = (8, 6, 5)
ROWS = (64, 48, 48)
TABLE = (1, 3, 0)
SLOTS = ((1, 2), (3, 4), (0,))
WIDE = (640, 640, 384)


def share_of(channels, n_dp):
    return channels // n_dp


def dot(a, b):
    return jnp.dot(a, b, preferred_element_type=F32)


def dot_nt(a, b):
    return lax.dot_general(a, b, (((1,), (1,)), ((), ())), preferred_element_type=F32)


def dot_tn(a, b):
    return lax.dot_general(a, b, (((0,), (0,)), ((), ())), preferred_element_type=F32)


def mix_flat(table, values):
    total = None
    for n in range(8):
        term = table(0, n)[None] * values(n)
        total = term if total is None else total + term
    return total


def mix_pair(table, t, plus_of, minus_of, back):
    plus = minus = None
    for n in range(8):
        c, q = table(t, n)[None], table(t + 1, n)[None]
        p, m = plus_of(n), minus_of(n)
        if back:
            up, um = c * p - q * m, q * p + c * m
        else:
            up, um = c * p + q * m, c * m - q * p
        plus = up if plus is None else plus + up
        minus = um if minus is None else minus + um
    return plus, minus


def kernel(
    n_dp, scale,
    h_in, g_in, w_in, radial_in, angle_in, atoms_in, ecount_in, acount_in, in_grad, wout,
    h, g0, w, radial, angle, atoms, ecount, acount,
    trig, tab_f, tab_b, hs1, hs2, hs0, y, summed, gates, sums, dref, ub1, ub2, ub0,
    rb1, rb2, rb0, ob1, ob2, ob0, fx, fb, frx, dwf,
    pk1, pk2, pk0, px1, px2, px0, st1, st2, st0, rs1, rs2, rs0,
    in_sem, ring_send, ring_recv, fin_send, fin_recv, pair_send, pair_recv, plane_send, plane_recv,
):
    hs, ub, rb, ob = (hs1, hs2, hs0), (ub1, ub2, ub0), (rb1, rb2, rb0), (ob1, ob2, ob0)
    pk, px, st, rs = (pk1, pk2, pk0), (px1, px2, px0), (st1, st2, st0), (rs1, rs2, rs0)
    batches, coeff_rows, atom_slots, channels = g0.shape
    edges = angle.shape[1]
    section = lax.axis_index("section")
    dp = lax.axis_index("dp")
    core = lax.rem(dp, 2)
    chip = dp // 2
    chips = n_dp // 2
    tiles = [pl.ds(LANES * j, LANES) for j in range(channels // LANES)]

    inputs = [
        pltpu.make_async_copy(src, dst, in_sem.at[n])
        for n, (src, dst) in enumerate(
            (
                (angle_in, angle),
                (atoms_in, atoms),
                (ecount_in, ecount),
                (radial_in, radial),
                (h_in.at[1], h.at[1]),
                (w_in.at[1], w.at[1]),
                (g_in, g0),
                (h_in.at[0], h.at[0]),
                (w_in.at[0], w.at[0]),
                (acount_in, acount),
            )
        )
    ]
    for copy in inputs:
        copy.start()

    barrier = pltpu.get_barrier_semaphore()
    for off in range(1, 4):
        pl.semaphore_signal(barrier, inc=1, device_id=(lax.rem(section + off, 4), dp), device_id_type=MESH)
    pl.semaphore_signal(barrier, inc=1, device_id=(section, dp + 1 - 2 * core), device_id_type=MESH)

    def greet(off, carry):
        peer = lax.rem(chip + off, chips) * 2 + core
        pl.semaphore_signal(barrier, inc=1, device_id=(section, peer), device_id_type=MESH)
        return carry

    lax.fori_loop(1, chips, greet, 0)

    for n in range(4):
        inputs[n].wait()
    turn = jnp.concatenate([angle[...], 2.0 * angle[...]], 0)
    trig[0] = jnp.cos(turn)
    trig[1] = jnp.sin(turn)

    def make_tables(b):
        dst = atoms[b, 0:1, :]
        src = atoms[b, 1:2, :]
        edge = lax.broadcasted_iota(jnp.int32, (1, edges), 1)
        live = jnp.where(edge < ecount[b], 0.25, 0.0).astype(F32)
        factors = [live]
        for m in range(2):
            for f in range(2):
                factors.append(live * trig[f, pl.ds(batches * m + b, 1), :])
        slot = lax.broadcasted_iota(jnp.int32, (64, edges), 0)
        for code, tab in ((src * 8 + dst, tab_f), (dst * 8 + src, tab_b)):
            hit = slot == code
            pick = jnp.concatenate([jnp.where(hit, f, 0.0) for f in factors], 0)
            high = pick.astype(BF16)
            low = (pick - high.astype(F32)).astype(BF16)
            rad = radial[b]
            tab[b] = (dot(high, rad) + dot(low, rad)).reshape(5, 8, 8, channels)

    def group_rows(v, k):
        v = v.astype(F32)
        if k == 2:
            v = jnp.concatenate([jnp.zeros((1, atom_slots, channels), F32), v], 0)
        return v.reshape(ROWS[k], channels)

    def prepare(p):
        lap = 1 - p // batches
        b = lax.rem(p, batches)

        @pl.when(p < batches)
        def _():
            make_tables(b)

        @pl.when(p == 0)
        def _():
            inputs[4].wait()
            inputs[5].wait()

        @pl.when(p == batches)
        def _():
            inputs[7].wait()
            inputs[8].wait()

        h0 = group_rows(h[lap, b, 0:5], 2).astype(BF16)
        hs0[lap, b] = h0
        y[0:6] = dot(h0, w[lap, 0]).reshape(6, 8, channels)
        for k, at in ((0, 6), (1, 14)):
            v = group_rows(h[lap, b, FIRST[k] : FIRST[k] + COUNT[k]], k)
            half = ROWS[k] // 2
            hs[k][lap, b] = v.astype(BF16)
            turned = jnp.concatenate([-v[half:], v[:half]], 0)
            pair = jnp.concatenate([v.astype(BF16), turned.astype(BF16)], 1)
            both = w[lap, SLOTS[k][0] : SLOTS[k][0] + 2].reshape(2 * channels, channels)
            y[at : at + COUNT[k]] = dot(pair, both).reshape(COUNT[k], 8, channels)
        for lanes in tiles:
            table = lambda t, n: tab_f[b, t, n, :, lanes]
            flat = mix_flat(table, lambda n: y[1:6, n : n + 1, lanes])
            summed[lap, b, 0:5, :, lanes] = flat
            gates[lap, b, :, lanes] = jax.nn.sigmoid(flat[0])
            for k, at in ((0, 6), (1, 14)):
                half = COUNT[k] // 2
                plus, minus = mix_pair(
                    table,
                    TABLE[k],
                    lambda n: y[at : at + half, n : n + 1, lanes],
                    lambda n: y[at + half : at + 2 * half, n : n + 1, lanes],
                    False,
                )
                summed[lap, b, FIRST[k] : FIRST[k] + half, :, lanes] = plus
                summed[lap, b, FIRST[k] + half : FIRST[k] + 2 * half, :, lanes] = minus

    def ring_copy(lap, b, k):
        slot = lap * batches + b
        there = jnp.where(section == 0, 0, lap) * batches + b
        return pltpu.make_async_remote_copy(
            src_ref=ob[k].at[slot],
            dst_ref=rb[k].at[there],
            send_sem=ring_send.at[k, slot],
            recv_sem=ring_recv.at[k, there],
            device_id=(lax.rem(section + 3, 4), dp),
            device_id_type=MESH,
        )

    def ring_arrival(lap, b, k):
        slot = lap * batches + b
        return pltpu.make_async_remote_copy(
            src_ref=ob[k].at[slot],
            dst_ref=rb[k].at[slot],
            send_sem=ring_send.at[k, slot],
            recv_sem=ring_recv.at[k, slot],
            device_id=(lax.rem(section + 3, 4), dp),
            device_id_type=MESH,
        )

    def final_copy(b, to):
        return pltpu.make_async_remote_copy(
            src_ref=fb.at[b, to],
            dst_ref=frx.at[b],
            send_sem=fin_send.at[b, to],
            recv_sem=fin_recv.at[b],
            device_id=(to, dp),
            device_id_type=MESH,
        )

    def unit(lap, b, k):
        slot = lap * batches + b
        count = COUNT[k]
        span = slice(FIRST[k], FIRST[k] + count)

        @pl.when((section == 3) & (lap == 1))
        def _():
            rb[k][slot] = group_rows(g0[b, span], k).astype(BF16)

        @pl.when((section != 3) | (lap == 0))
        def _():
            ring_arrival(lap, b, k).wait_recv()

        pad = ROWS[k] // 8 - count
        for lanes in tiles:
            g = rb[k][slot, :, lanes].astype(F32).reshape(ROWS[k] // 8, 8, LANES)[pad:]
            gate = gates[lap, b, :, lanes]
            partial = jnp.sum(g * summed[lap, b, span, :, lanes], 0)
            dref[0:count, :, lanes] = g * gate[None]
            if k == 0:
                sums[b, :, lanes] = partial
            elif k == 1:
                sums[b, :, lanes] += partial
            else:
                extra = (sums[b, :, lanes] + partial) * gate * (1.0 - gate)
                dref[0, :, lanes] += extra
        for j, lanes in enumerate(tiles):
            table = lambda t, n: tab_b[b, t, n, :, lanes]
            if k == 2:
                flat = mix_flat(table, lambda n: dref[0:5, n : n + 1, lanes])
                flat = jnp.concatenate([jnp.zeros((8, LANES), F32), flat.reshape(40, LANES)], 0)
                ub0[lap, b, :, lanes] = flat.astype(BF16)
            else:
                half = count // 2
                up, um = mix_pair(
                    table,
                    TABLE[k],
                    lambda n: dref[0:half, n : n + 1, lanes],
                    lambda n: dref[half : 2 * half, n : n + 1, lanes],
                    True,
                )
                up = up.reshape(-1, LANES)
                um = um.reshape(-1, LANES)
                later = pl.ds(channels + LANES * j, LANES)
                ub[k][lap, b, :, lanes] = jnp.concatenate([up, um], 0).astype(BF16)
                ub[k][lap, b, :, later] = jnp.concatenate([um, -up], 0).astype(BF16)
        if k == 2:
            weight = w[lap, 0]
        else:
            weight = jnp.concatenate([w[lap, SLOTS[k][0]], w[lap, SLOTS[k][1]]], 1)
        out = rb[k][slot].astype(F32) + dot_nt(ub[k][lap, b], weight)
        ob[k][slot] = out.astype(BF16)

        @pl.when((section != 0) | (lap == 1))
        def _():
            ring_copy(lap, b, k).start()

    def finish(b):
        for j, lanes in enumerate(tiles):
            fx[j, 0:40] = ob0[b, :, lanes].astype(F32)[8:]
            fx[j, 40:104] = ob1[b, :, lanes].astype(F32)
            fx[j, 104:152] = ob2[b, :, lanes].astype(F32)
        for to in range(4):
            for n in range(2):
                atom = 2 * to + n
                keep = jnp.where(acount[b] > atom, 1.0, 0.0).astype(F32)
                for j, lanes in enumerate(tiles):
                    part = fx[j, pl.ds(atom, coeff_rows, stride=8), :] * keep
                    fb[b, to, n, 0:coeff_rows, lanes] = part.astype(BF16)
        for to in range(1, 4):
            final_copy(b, to).start()

    def pair_copy(lap, k):
        return pltpu.make_async_remote_copy(
            src_ref=pk[k].at[lap, 1 - core],
            dst_ref=px[k].at[lap],
            send_sem=pair_send.at[k, lap],
            recv_sem=pair_recv.at[k, lap],
            device_id=(section, dp + 1 - 2 * core),
            device_id_type=MESH,
        )

    def weight_term(lap, k):
        left = hs[k][lap].reshape(batches * ROWS[k], channels)
        right = ub[k][lap].reshape(batches * ROWS[k], -1)
        grads = dot_tn(left, right)
        for n in range(len(SLOTS[k])):
            dwf[n] = grads[:, channels * n : channels * (n + 1)]
        low = lax.broadcasted_iota(jnp.int32, (8, channels), 0) < 4

        def pack(j, carry):
            t = [
                [dwf[n, pl.ds(pl.multiple_of(24 * j + 8 * i, 8), 8), :] for i in range(3)]
                for n in range(len(SLOTS[k]))
            ]
            if k == 2:
                blocks = (
                    jnp.concatenate([t[0][0], t[0][1]], 0),
                    jnp.concatenate([t[0][2], pltpu.roll(t[0][1], 4, 0)], 0),
                )
            else:
                blocks = []
                for c in range(2):
                    if c == 0:
                        mixed = jnp.where(low, t[0][1], pltpu.roll(t[1][1], 4, 0))
                    else:
                        mixed = jnp.where(low, pltpu.roll(t[0][1], 4, 0), t[1][1])
                    whole = jnp.concatenate([t[0][2 * c], t[1][2 * c]], 0)
                    last = jnp.concatenate([mixed[:, 256:], jnp.zeros((8, LANES), F32)], 1)
                    blocks.append(
                        jnp.concatenate([whole, jnp.concatenate([mixed[:, :256], last], 0)], 1)
                    )
            for c in range(2):
                pk[k][lap, c, j] = blocks[c].astype(BF16)
            return carry

        lax.fori_loop(0, chips, pack, 0)
        pair_copy(lap, k).start()

    def plane_copy(lap, k, to):
        return pltpu.make_async_remote_copy(
            src_ref=st[k].at[lap, to],
            dst_ref=rs[k].at[lap, chip],
            send_sem=plane_send.at[k, lap, to],
            recv_sem=plane_recv.at[k, lap, chip],
            device_id=(section, to * 2 + core),
            device_id_type=MESH,
        )

    def plane_arrival(lap, k, source):
        return pltpu.make_async_remote_copy(
            src_ref=st[k].at[lap, source],
            dst_ref=rs[k].at[lap, source],
            send_sem=plane_send.at[k, lap, source],
            recv_sem=plane_recv.at[k, lap, source],
            device_id=(section, source * 2 + core),
            device_id_type=MESH,
        )

    def spread(lap, k):
        pair_copy(lap, k).wait_recv()

        def add(off, carry):
            j = lax.rem(chip + off, chips)
            st[k][lap, j] = (pk[k][lap, core, j].astype(F32) + px[k][lap, j].astype(F32)).astype(BF16)

            @pl.when(off < chips)
            def _():
                plane_copy(lap, k, j).start()

            return carry

        lax.fori_loop(1, chips + 1, add, 0)

    def collect(lap, k):
        def take(off, total):
            j = lax.rem(chip + off, chips)
            plane_arrival(lap, k, j).wait_recv()
            return total + rs[k][lap, j].astype(F32)

        total = lax.fori_loop(1, chips, take, st[k][lap, chip].astype(F32)) * scale
        if k == 2:
            parts = [(0, total[0:8], total[8:12])]
        else:
            mixed = jnp.concatenate([total[0:8, channels:], total[8:16, channels : channels + LANES]], 1)
            parts = [
                (SLOTS[k][0], total[0:8, :channels], mixed[0:4]),
                (SLOTS[k][1], total[8:16, :channels], mixed[4:8]),
            ]
        for slot, whole, part in parts:

            @pl.when(core == 0)
            def _():
                wout[lap, slot, 0:8] = whole
                wout[lap, slot, 8:12] = part

            @pl.when(core == 1)
            def _():
                wout[lap, slot, 0:4] = part
                wout[lap, slot, 4:12] = whole

    @pl.when(section == 0)
    def _():
        fb[...] = jnp.zeros_like(fb)

    def prepare_range(lo, hi):
        def one(p, carry):
            prepare(p)
            return carry

        lax.fori_loop(lo, hi, one, 0)

    ahead = jnp.where(section == 3, 1, jnp.where(section == 2, batches, 2 * batches))
    prepare_range(0, ahead)
    inputs[6].wait()
    inputs[9].wait()
    pl.semaphore_wait(barrier, 4 + chips - 1)

    def run_lap(turn_index, carry):
        lap = 1 - turn_index

        def first(b, carry):
            now = jnp.where(section == 3, batches * turn_index + b, batches)
            until = jnp.where(section == 3, now + 1, batches + batches)
            late = (section == 3) & (lap == 1) & (b >= 1)
            fill = (section >= 2) & (lap == 0) & (b == 0)
            lo = jnp.where(fill, batches, now)
            hi = jnp.where(fill, 2 * batches, jnp.where(late, until, lo))
            prepare_range(lo, hi)
            unit(lap, b, 0)
            return carry

        lax.fori_loop(0, batches, first, 0)
        weight_term(lap, 0)

        def second(b, carry):
            unit(lap, b, 1)

            @pl.when(b == 1)
            def _():
                spread(lap, 0)

            return carry

        lax.fori_loop(0, batches, second, 0)
        weight_term(lap, 1)

        def third(b, carry):
            unit(lap, b, 2)

            @pl.when((section == 0) & (lap == 0))
            def _():
                finish(b)

            @pl.when(b == 1)
            def _():
                spread(lap, 1)

            return carry

        lax.fori_loop(0, batches, third, 0)
        weight_term(lap, 2)
        spread(lap, 2)
        return carry

    lax.fori_loop(0, 2, run_lap, 0)
    for lap, k in ((1, 0), (1, 1), (1, 2), (0, 0), (0, 1)):
        collect(lap, k)

    @pl.when(section == 0)
    def _():
        for b in range(batches):
            in_grad[b] = fb[b, 0]
            for to in range(1, 4):
                final_copy(b, to).wait_send()

    @pl.when(section != 0)
    def _():
        for b in range(batches):
            final_copy(b, section).wait_recv()
            in_grad[b] = frx[b]

    def ring_left(i, carry):
        lap = 1 - i // batches

        @pl.when((section != 0) | (lap == 1))
        def _():
            for k in range(3):
                ring_copy(lap, lax.rem(i, batches), k).wait_send()

        return carry

    lax.fori_loop(0, 2 * batches, ring_left, 0)
    for lap in (1, 0):
        for k in range(3):
            pair_copy(lap, k).wait_send()

            def left(off, carry):
                plane_copy(lap, k, lax.rem(chip + off, chips)).wait_send()
                return carry

            lax.fori_loop(1, chips, left, 0)
    collect(0, 2)


def body(n_dp, h_saved, out_cot, so2_weight, radial, edge_angle, edge_atoms, edge_count, atom_count):
    batches, atom_slots, coeff_rows, channels = out_cot.shape
    edges = edge_angle.shape[1]
    share = share_of(channels, n_dp)
    chips = n_dp // 2
    slots = 2 * batches
    scale = 1.0 / math.sqrt(n_dp * batches * edges)
    vmem = pl.BlockSpec(memory_space=pltpu.VMEM)
    dma = pltpu.SemaphoreType.DMA
    h = h_saved[:, 0].transpose(0, 1, 3, 2, 4)
    g0 = out_cot.transpose(0, 2, 1, 3)
    w = so2_weight[:, 0]
    args = (h, g0, w, radial, edge_angle, edge_atoms, edge_count, atom_count)
    homes = [pltpu.VMEM(a.shape, a.dtype) for a in args[:6]] + [pltpu.SMEM(a.shape, a.dtype) for a in args[6:]]
    in_grad, wout = pl.pallas_call(
        functools.partial(kernel, n_dp, scale),
        out_shape=(
            jax.ShapeDtypeStruct((batches, 2, 32, channels), BF16),
            jax.ShapeDtypeStruct((2, 5, share, channels), F32),
        ),
        in_specs=[pl.BlockSpec(memory_space=pl.ANY)] * 8,
        out_specs=(vmem, vmem),
        scratch_shapes=homes
        + [
            pltpu.VMEM((2, 2 * batches, edges), F32),
            pltpu.VMEM((batches, 5, 8, 8, channels), F32),
            pltpu.VMEM((batches, 5, 8, 8, channels), F32),
        ]
        + [pltpu.VMEM((2, batches, r, channels), BF16) for r in ROWS]
        + [
            pltpu.VMEM((20, 8, channels), F32),
            pltpu.VMEM((2, batches, coeff_rows, 8, channels), F32),
            pltpu.VMEM((2, batches, 8, channels), F32),
            pltpu.VMEM((batches, 8, channels), F32),
            pltpu.VMEM((8, 8, channels), F32),
            pltpu.VMEM((2, batches, ROWS[0], 2 * channels), BF16),
            pltpu.VMEM((2, batches, ROWS[1], 2 * channels), BF16),
            pltpu.VMEM((2, batches, ROWS[2], channels), BF16),
        ]
        + [pltpu.VMEM((slots, r, channels), BF16) for r in ROWS]
        + [pltpu.VMEM((slots, r, channels), BF16) for r in ROWS]
        + [
            pltpu.VMEM((channels // LANES, 152, LANES), F32),
            pltpu.VMEM((batches, 4, 2, 32, channels), BF16),
            pltpu.VMEM((batches, 2, 32, channels), BF16),
            pltpu.VMEM((2, channels, channels), F32),
        ]
        + [pltpu.VMEM((2, 2, chips, 16, n), BF16) for n in WIDE]
        + [pltpu.VMEM((2, chips, 16, n), BF16) for n in WIDE]
        + [pltpu.VMEM((2, chips, 16, n), BF16) for n in WIDE]
        + [pltpu.VMEM((2, chips, 16, n), BF16) for n in WIDE]
        + [
            dma((10,)),
            dma((3, slots)),
            dma((3, slots)),
            dma((batches, 4)),
            dma((batches,)),
            dma((3, 2)),
            dma((3, 2)),
            dma((3, 2, chips)),
            dma((3, 2, chips)),
        ],
        compiler_params=pltpu.CompilerParams(
            collective_id=0, has_side_effects=True, vmem_limit_bytes=60 * 1024 * 1024
        ),
        name="window_backward",
    )(*args)
    in_grad = in_grad[:, :, :coeff_rows]
    return in_grad, wout[:, None]


def solution(mesh):
    placed = (
        P(None, "section", "dp", None, None, None),
        P("dp", None, None, None),
        P(None, "section", None, None, None),
        P("dp", None, None),
        P("dp", None),
        P("dp", None, None),
        P("dp"),
        P("dp"),
    )
    return jax.shard_map(
        functools.partial(body, mesh.shape["dp"]),
        mesh=mesh,
        in_specs=placed,
        out_specs=(P("dp", "section", None, None), P(None, "section", None, "dp", None)),
        check_vma=False,
    )
```

time: 75.9 us -> 60 us (0.79)
  Pallas kernels: 69.6 us -> 55.7 us
  local copies, waits for them, and re-layouts: 5.34 us -> 3.48 us
    pallas_call x1, Pallas kernels: 69.6 us -> 55.7 us  [body(): pl.pallas_call(functools.partial(kernel, n_dp, scale), out_shape=(jax.Sha...]
    unnamed x14 -> x2, local copies, waits for them, and re-layouts: 5.18 us -> 2.54 us
    slice x1, local copies, waits for them, and re-layouts: 0.02 us -> 0.93 us  [body(): in_grad = in_grad[:, :, :coeff_rows]]
where the time goes in v2:
time: 60 us; the launch traced here: 59.9 us
  Pallas kernels  55.7 us (93%)
  local copies, waits for them, and re-layouts  3.48 us (6%)
  between operations  0.64 us (1%)
    pallas_call x1, Pallas kernels, body(): pl.pallas_call(functools.partial(kernel, n_dp, scale), out_shape=(jax.Sha...  55.7 us
    unnamed x2, local copies, waits for them, and re-layouts  2.54 us

profile of v2, /device:TPU:1, one launch (start us, length us, event | category | flops | bytes accessed | tf_op | source)
XLA Modules:
  0.0 59.9 jit_solution(18002940053950422086)
XLA Ops:
  0.6 55.7 %window_backward.1 = (bf16[4,2,32,384]{3,2,1,0:T(8,128)(2,1)}, f32[2,5,12,384]{3,2,1,0:T(8,128)}) custom-call(bf16[2,4,19,8,384]{4,3,2,1,0:T(8,128)(2,1)} %bitcast.7, bf16[4,19,8,384]{3,2,1,0:T(8,128)(2,1)} %bitcast.8, bf16[2,5,384,384]{3,2,1,0:T(8,128)(2,1)} %bitcast.6, bf16[4,112,384]{2,1,0:T(8,128)(2,1)} %radial_in.1, f32[4,112]{1,0:T(4,128)} %angle_in.1, ...), custom_call_target="tpu_custom_call" | custom-call | tf_op jit(solution)/shard_map/window_backward/pallas_call | solution.py:521
  56.4 0.9 %slice.3 = bf16[4,2,19,384]{3,2,1,0:T(8,128)(2,1)S(1)} slice(bf16[4,2,32,384]{3,2,1,0:T(8,128)(2,1)} %get-tuple-element.4), slice={[0:4], [0:2], [0:19], [0:384]} | slice | bytes 233472 | tf_op jit(solution)/shard_map/slice | solution.py:574
  57.3 0.7 %copy.10 = bf16[4,2,19,384]{3,1,2,0:T(2,128)(2,1)} copy(bf16[4,2,19,384]{3,2,1,0:T(8,128)(2,1)S(1)} %slice.3) | data formatting | bytes 233472
  58.0 1.8 %copy.11 = f32[2,1,5,12,384]{4,1,3,2,0:T(1,128)} copy(f32[2,1,5,12,384]{4,3,2,0,1:T(8,128)} %bitcast.9) | data formatting | bytes 368640

commit v3 on v2

--- a/solution.py
+++ b/solution.py
@@ -12,8 +12,16 @@
 BF16 = jnp.bfloat16
 MESH = pl.DeviceIdType.MESH
 LANES = 128
-FIRST = (5, 13, 0)
-COUNT = (8, 6, 5)
+COEFFS = (
+    ((5, 6, 9, 10), (7, 8, 11, 12)),
+    ((13, 14, 16, 17), (15, 18)),
+    ((3, 4), (0, 1, 2)),
+)
+UNITS = tuple((k, m) for k in range(3) for m in range(2))
+UNIT_ROWS = (32, 32, 32, 16, 16, 32)
+OFFSET = (0, 32, 0, 32, 0, 16)
+BASE = (0, 4, 8, 12, 14, 16)
+IN_Y = (0, 4, 8, 12, 14, 17)
 ROWS = (64, 48, 48)
 TABLE = (1, 3, 0)
 SLOTS = ((1, 2), (3, 4), (0,))
@@ -26,10 +34,6 @@
 
 def dot(a, b):
     return jnp.dot(a, b, preferred_element_type=F32)
-
-
-def dot_nt(a, b):
-    return lax.dot_general(a, b, (((1,), (1,)), ((), ())), preferred_element_type=F32)
 
 
 def dot_tn(a, b):
@@ -62,12 +66,13 @@
     n_dp, scale,
     h_in, g_in, w_in, radial_in, angle_in, atoms_in, ecount_in, acount_in, in_grad, wout,
     h, g0, w, radial, angle, atoms, ecount, acount,
-    trig, tab_f, tab_b, hs1, hs2, hs0, y, summed, gates, sums, dref, ub1, ub2, ub0,
-    rb1, rb2, rb0, ob1, ob2, ob0, fx, fb, frx, dwf,
+    wt, trig, tab_f, tab_b, hs1, hs2, hs0, y, summed, gates, sums, dref, ub1, ub2, ub0,
+    rb_0, rb_1, rb_2, rb_3, rb_4, rb_5, ob, fx, fy, fb, frx, dwf,
     pk1, pk2, pk0, px1, px2, px0, st1, st2, st0, rs1, rs2, rs0,
     in_sem, ring_send, ring_recv, fin_send, fin_recv, pair_send, pair_recv, plane_send, plane_recv,
 ):
-    hs, ub, rb, ob = (hs1, hs2, hs0), (ub1, ub2, ub0), (rb1, rb2, rb0), (ob1, ob2, ob0)
+    hs, ub = (hs1, hs2, hs0), (ub1, ub2, ub0)
+    rb = (rb_0, rb_1, rb_2, rb_3, rb_4, rb_5)
     pk, px, st, rs = (pk1, pk2, pk0), (px1, px2, px0), (st1, st2, st0), (rs1, rs2, rs0)
     batches, coeff_rows, atom_slots, channels = g0.shape
     edges = angle.shape[1]
@@ -134,11 +139,19 @@
             rad = radial[b]
             tab[b] = (dot(high, rad) + dot(low, rad)).reshape(5, 8, 8, channels)
 
-    def group_rows(v, k):
-        v = v.astype(F32)
-        if k == 2:
-            v = jnp.concatenate([jnp.zeros((1, atom_slots, channels), F32), v], 0)
-        return v.reshape(ROWS[k], channels)
+    def picked(ref, lap_or_none, b, coeffs):
+        parts = []
+        for k in coeffs:
+            if k is None:
+                parts.append(jnp.zeros((atom_slots, channels), F32))
+            else:
+                row = ref[b, abs(k)] if lap_or_none is None else ref[lap_or_none, b, abs(k)]
+                parts.append(-row.astype(F32) if k < 0 else row.astype(F32))
+        return jnp.concatenate(parts, 0)
+
+    def turn_weights(lap):
+        for n in range(5):
+            wt[lap, channels * n : channels * (n + 1)] = w[lap, n].T
 
     def prepare(p):
         lap = 1 - p // batches
@@ -152,47 +165,57 @@
         def _():
             inputs[4].wait()
             inputs[5].wait()
-
-        @pl.when(p == batches)
-        def _():
+            turn_weights(1)
             inputs[7].wait()
             inputs[8].wait()
-
-        h0 = group_rows(h[lap, b, 0:5], 2).astype(BF16)
+            turn_weights(0)
+
+        h0 = picked(h, lap, b, COEFFS[2][0] + (None,) + COEFFS[2][1]).astype(BF16)
         hs0[lap, b] = h0
-        y[0:6] = dot(h0, w[lap, 0]).reshape(6, 8, channels)
-        for k, at in ((0, 6), (1, 14)):
-            v = group_rows(h[lap, b, FIRST[k] : FIRST[k] + COUNT[k]], k)
-            half = ROWS[k] // 2
-            hs[k][lap, b] = v.astype(BF16)
-            turned = jnp.concatenate([-v[half:], v[:half]], 0)
-            pair = jnp.concatenate([v.astype(BF16), turned.astype(BF16)], 1)
+        y[14:20] = dot(h0, w[lap, 0]).reshape(6, 8, channels)
+        for k, at in ((0, 0), (1, 8)):
+            straight = COEFFS[k][0] + COEFFS[k][1]
+            turned = []
+            for coeffs in COEFFS[k]:
+                half = len(coeffs) // 2
+                turned += [-c for c in coeffs[half:]] + list(coeffs[:half])
+            v = picked(h, lap, b, straight).astype(BF16)
+            hs[k][lap, b] = v
+            pair = jnp.concatenate([v, picked(h, lap, b, turned).astype(BF16)], 1)
             both = w[lap, SLOTS[k][0] : SLOTS[k][0] + 2].reshape(2 * channels, channels)
-            y[at : at + COUNT[k]] = dot(pair, both).reshape(COUNT[k], 8, channels)
+            y[at : at + len(straight)] = dot(pair, both).reshape(len(straight), 8, channels)
         for lanes in tiles:
             table = lambda t, n: tab_f[b, t, n, :, lanes]
-            flat = mix_flat(table, lambda n: y[1:6, n : n + 1, lanes])
-            summed[lap, b, 0:5, :, lanes] = flat
-            gates[lap, b, :, lanes] = jax.nn.sigmoid(flat[0])
-            for k, at in ((0, 6), (1, 14)):
-                half = COUNT[k] // 2
+            for u, (k, m) in enumerate(UNITS):
+                count = len(COEFFS[k][m])
+                at, to = IN_Y[u], BASE[u]
+                if k == 2:
+                    flat = mix_flat(table, lambda n: y[at : at + count, n : n + 1, lanes])
+                    summed[lap, b, to : to + count, :, lanes] = flat
+                    if m == 1:
+                        gates[lap, b, :, lanes] = jax.nn.sigmoid(flat[0])
+                    continue
+                half = count // 2
                 plus, minus = mix_pair(
                     table,
                     TABLE[k],
                     lambda n: y[at : at + half, n : n + 1, lanes],
-                    lambda n: y[at + half : at + 2 * half, n : n + 1, lanes],
+                    lambda n: y[at + half : at + count, n : n + 1, lanes],
                     False,
                 )
-                summed[lap, b, FIRST[k] : FIRST[k] + half, :, lanes] = plus
-                summed[lap, b, FIRST[k] + half : FIRST[k] + 2 * half, :, lanes] = minus
+                summed[lap, b, to : to + half, :, lanes] = plus
+                summed[lap, b, to + half : to + count, :, lanes] = minus
+
+    def sent(lap, b, u):
+        start = pl.multiple_of(b * sum(UNIT_ROWS) + sum(UNIT_ROWS[:u]), 16)
+        return ob.at[lap, pl.ds(start, UNIT_ROWS[u])]
 
     def ring_copy(lap, b, k):
-        slot = lap * batches + b
         there = jnp.where(section == 0, 0, lap) * batches + b
         return pltpu.make_async_remote_copy(
-            src_ref=ob[k].at[slot],
+            src_ref=sent(lap, b, k),
             dst_ref=rb[k].at[there],
-            send_sem=ring_send.at[k, slot],
+            send_sem=ring_send.at[lap],
             recv_sem=ring_recv.at[k, there],
             device_id=(lax.rem(section + 3, 4), dp),
             device_id_type=MESH,
@@ -201,9 +224,9 @@
     def ring_arrival(lap, b, k):
         slot = lap * batches + b
         return pltpu.make_async_remote_copy(
-            src_ref=ob[k].at[slot],
+            src_ref=sent(lap, b, k),
             dst_ref=rb[k].at[slot],
-            send_sem=ring_send.at[k, slot],
+            send_sem=ring_send.at[lap],
             recv_sem=ring_recv.at[k, slot],
             device_id=(lax.rem(section + 3, 4), dp),
             device_id_type=MESH,
@@ -213,34 +236,37 @@
         return pltpu.make_async_remote_copy(
             src_ref=fb.at[b, to],
             dst_ref=frx.at[b],
-            send_sem=fin_send.at[b, to],
+            send_sem=fin_send.at[0],
             recv_sem=fin_recv.at[b],
             device_id=(to, dp),
             device_id_type=MESH,
         )
 
-    def unit(lap, b, k):
+    def unit(lap, b, u):
         slot = lap * batches + b
-        count = COUNT[k]
-        span = slice(FIRST[k], FIRST[k] + count)
+        k, m = UNITS[u]
+        coeffs = COEFFS[k][m]
+        count = len(coeffs)
+        pad = UNIT_ROWS[u] // 8 - count
+        span = slice(BASE[u], BASE[u] + count)
+        rows = slice(OFFSET[u], OFFSET[u] + UNIT_ROWS[u])
 
         @pl.when((section == 3) & (lap == 1))
         def _():
-            rb[k][slot] = group_rows(g0[b, span], k).astype(BF16)
+            rb[u][slot] = picked(g0, None, b, (None,) * pad + coeffs).astype(BF16)
 
         @pl.when((section != 3) | (lap == 0))
         def _():
-            ring_arrival(lap, b, k).wait_recv()
-
-        pad = ROWS[k] // 8 - count
+            ring_arrival(lap, b, u).wait_recv()
+
         for lanes in tiles:
-            g = rb[k][slot, :, lanes].astype(F32).reshape(ROWS[k] // 8, 8, LANES)[pad:]
+            g = rb[u][slot, :, lanes].astype(F32).reshape(UNIT_ROWS[u] // 8, 8, LANES)[pad:]
             gate = gates[lap, b, :, lanes]
             partial = jnp.sum(g * summed[lap, b, span, :, lanes], 0)
             dref[0:count, :, lanes] = g * gate[None]
-            if k == 0:
+            if u == 0:
                 sums[b, :, lanes] = partial
-            elif k == 1:
+            elif u < len(UNITS) - 1:
                 sums[b, :, lanes] += partial
             else:
                 extra = (sums[b, :, lanes] + partial) * gate * (1.0 - gate)
@@ -248,48 +274,55 @@
         for j, lanes in enumerate(tiles):
             table = lambda t, n: tab_b[b, t, n, :, lanes]
             if k == 2:
-                flat = mix_flat(table, lambda n: dref[0:5, n : n + 1, lanes])
-                flat = jnp.concatenate([jnp.zeros((8, LANES), F32), flat.reshape(40, LANES)], 0)
-                ub0[lap, b, :, lanes] = flat.astype(BF16)
+                flat = mix_flat(table, lambda n: dref[0:count, n : n + 1, lanes]).reshape(8 * count, LANES)
+                if pad:
+                    flat = jnp.concatenate([jnp.zeros((8 * pad, LANES), F32), flat], 0)
+                ub0[lap, b, rows, lanes] = flat.astype(BF16)
             else:
                 half = count // 2
                 up, um = mix_pair(
                     table,
                     TABLE[k],
                     lambda n: dref[0:half, n : n + 1, lanes],
-                    lambda n: dref[half : 2 * half, n : n + 1, lanes],
+                    lambda n: dref[half:count, n : n + 1, lanes],
                     True,
                 )
                 up = up.reshape(-1, LANES)
                 um = um.reshape(-1, LANES)
                 later = pl.ds(channels + LANES * j, LANES)
-                ub[k][lap, b, :, lanes] = jnp.concatenate([up, um], 0).astype(BF16)
-                ub[k][lap, b, :, later] = jnp.concatenate([um, -up], 0).astype(BF16)
-        if k == 2:
-            weight = w[lap, 0]
-        else:
-            weight = jnp.concatenate([w[lap, SLOTS[k][0]], w[lap, SLOTS[k][1]]], 1)
-        out = rb[k][slot].astype(F32) + dot_nt(ub[k][lap, b], weight)
-        ob[k][slot] = out.astype(BF16)
+                ub[k][lap, b, rows, lanes] = jnp.concatenate([up, um], 0).astype(BF16)
+                ub[k][lap, b, rows, later] = jnp.concatenate([um, -up], 0).astype(BF16)
+        first_slot, n_slots = SLOTS[k][0], len(SLOTS[k])
+        weight = wt[lap, channels * first_slot : channels * (first_slot + n_slots)]
+        out = rb[u][slot].astype(F32) + dot(ub[k][lap, b, rows], weight)
+        sent(lap, b, u)[...] = out.astype(BF16)
 
         @pl.when((section != 0) | (lap == 1))
         def _():
-            ring_copy(lap, b, k).start()
+            ring_copy(lap, b, u).start()
 
     def finish(b):
         for j, lanes in enumerate(tiles):
-            fx[j, 0:40] = ob0[b, :, lanes].astype(F32)[8:]
-            fx[j, 40:104] = ob1[b, :, lanes].astype(F32)
-            fx[j, 104:152] = ob2[b, :, lanes].astype(F32)
+            for u, (k, m) in enumerate(UNITS):
+                coeffs = COEFFS[k][m]
+                v = sent(0, b, u)[:, lanes].astype(F32)[UNIT_ROWS[u] - 8 * len(coeffs) :]
+                for n, c in enumerate(coeffs):
+                    fx[j, 8 * c : 8 * c + 8] = v[8 * n : 8 * n + 8]
         for to in range(4):
-            for n in range(2):
-                atom = 2 * to + n
-                keep = jnp.where(acount[b] > atom, 1.0, 0.0).astype(F32)
-                for j, lanes in enumerate(tiles):
+            for j, lanes in enumerate(tiles):
+                for n in range(2):
+                    atom = 2 * to + n
+                    keep = jnp.where(acount[b] > atom, 1.0, 0.0).astype(F32)
                     part = fx[j, pl.ds(atom, coeff_rows, stride=8), :] * keep
-                    fb[b, to, n, 0:coeff_rows, lanes] = part.astype(BF16)
+                    fy[j, pl.ds(n, coeff_rows, stride=2), :] = part
+                fb[b, to, :, lanes] = fy[j].astype(BF16)
         for to in range(1, 4):
             final_copy(b, to).start()
+
+    def deliver(b, source):
+        v = source.astype(F32)
+        for k in range(coeff_rows):
+            in_grad[b, k] = v[2 * k : 2 * k + 2].astype(BF16)
 
     def pair_copy(lap, k):
         return pltpu.make_async_remote_copy(
@@ -335,28 +368,21 @@
                 pk[k][lap, c, j] = blocks[c].astype(BF16)
             return carry
 
-        lax.fori_loop(0, chips, pack, 0)
+        lax.fori_loop(0, chips, pack, 0, unroll=min(4, chips))
         pair_copy(lap, k).start()
 
     def plane_copy(lap, k, to):
         return pltpu.make_async_remote_copy(
             src_ref=st[k].at[lap, to],
             dst_ref=rs[k].at[lap, chip],
-            send_sem=plane_send.at[k, lap, to],
-            recv_sem=plane_recv.at[k, lap, chip],
+            send_sem=plane_send.at[k, lap],
+            recv_sem=plane_recv.at[k, lap],
             device_id=(section, to * 2 + core),
             device_id_type=MESH,
         )
 
-    def plane_arrival(lap, k, source):
-        return pltpu.make_async_remote_copy(
-            src_ref=st[k].at[lap, source],
-            dst_ref=rs[k].at[lap, source],
-            send_sem=plane_send.at[k, lap, source],
-            recv_sem=plane_recv.at[k, lap, source],
-            device_id=(section, source * 2 + core),
-            device_id_type=MESH,
-        )
+    def await_bytes(ref, sem):
+        pltpu.make_async_copy(ref, ref, sem).wait()
 
     def spread(lap, k):
         pair_copy(lap, k).wait_recv()
@@ -364,22 +390,19 @@
         def add(off, carry):
             j = lax.rem(chip + off, chips)
             st[k][lap, j] = (pk[k][lap, core, j].astype(F32) + px[k][lap, j].astype(F32)).astype(BF16)
-
-            @pl.when(off < chips)
-            def _():
-                plane_copy(lap, k, j).start()
-
+            plane_copy(lap, k, j).start()
             return carry
 
-        lax.fori_loop(1, chips + 1, add, 0)
+        lax.fori_loop(1, chips, add, 0, unroll=min(5, chips - 1))
+        own = (pk[k][lap, core, chip].astype(F32) + px[k][lap, chip].astype(F32)).astype(BF16)
+        rs[k][lap, chip] = own
 
     def collect(lap, k):
-        def take(off, total):
-            j = lax.rem(chip + off, chips)
-            plane_arrival(lap, k, j).wait_recv()
-            return total + rs[k][lap, j].astype(F32)
-
-        total = lax.fori_loop(1, chips, take, st[k][lap, chip].astype(F32)) * scale
+        await_bytes(rs[k].at[lap, 0 : chips - 1], plane_recv.at[k, lap])
+        total = rs[k][lap, 0].astype(F32)
+        for j in range(1, chips):
+            total = total + rs[k][lap, j].astype(F32)
+        total = total * scale
         if k == 2:
             parts = [(0, total[0:8], total[8:12])]
         else:
@@ -392,17 +415,19 @@
 
             @pl.when(core == 0)
             def _():
-                wout[lap, slot, 0:8] = whole
-                wout[lap, slot, 8:12] = part
+                for n in range(8):
+                    wout[lap, slot, n] = whole[n : n + 1]
+                for n in range(4):
+                    wout[lap, slot, 8 + n] = part[n : n + 1]
 
             @pl.when(core == 1)
             def _():
-                wout[lap, slot, 0:4] = part
-                wout[lap, slot, 4:12] = whole
-
-    @pl.when(section == 0)
-    def _():
-        fb[...] = jnp.zeros_like(fb)
+                for n in range(4):
+                    wout[lap, slot, n] = part[n : n + 1]
+                for n in range(8):
+                    wout[lap, slot, 4 + n] = whole[n : n + 1]
+
+    fy[...] = jnp.zeros_like(fy)
 
     def prepare_range(lo, hi):
         def one(p, carry):
@@ -411,7 +436,7 @@
 
         lax.fori_loop(lo, hi, one, 0)
 
-    ahead = jnp.where(section == 3, 1, jnp.where(section == 2, batches, 2 * batches))
+    ahead = jnp.where(section == 3, 2, jnp.where(section == 2, batches, 2 * batches))
     prepare_range(0, ahead)
     inputs[6].wait()
     inputs[9].wait()
@@ -423,19 +448,21 @@
         def first(b, carry):
             now = jnp.where(section == 3, batches * turn_index + b, batches)
             until = jnp.where(section == 3, now + 1, batches + batches)
-            late = (section == 3) & (lap == 1) & (b >= 1)
+            late = (section == 3) & (lap == 1) & (b >= 2)
             fill = (section >= 2) & (lap == 0) & (b == 0)
             lo = jnp.where(fill, batches, now)
             hi = jnp.where(fill, 2 * batches, jnp.where(late, until, lo))
             prepare_range(lo, hi)
             unit(lap, b, 0)
+            unit(lap, b, 1)
             return carry
 
         lax.fori_loop(0, batches, first, 0)
         weight_term(lap, 0)
 
         def second(b, carry):
-            unit(lap, b, 1)
+            unit(lap, b, 2)
+            unit(lap, b, 3)
 
             @pl.when(b == 1)
             def _():
@@ -447,9 +474,10 @@
         weight_term(lap, 1)
 
         def third(b, carry):
-            unit(lap, b, 2)
-
-            @pl.when((section == 0) & (lap == 0))
+            unit(lap, b, 4)
+            unit(lap, b, 5)
+
+            @pl.when((section == 0) & (lap == 0) & (b < batches - 1))
             def _():
                 finish(b)
 
@@ -461,6 +489,11 @@
 
         lax.fori_loop(0, batches, third, 0)
         weight_term(lap, 2)
+
+        @pl.when((section == 0) & (lap == 0))
+        def _():
+            finish(batches - 1)
+
         spread(lap, 2)
         return carry
 
@@ -468,40 +501,31 @@
     for lap, k in ((1, 0), (1, 1), (1, 2), (0, 0), (0, 1)):
         collect(lap, k)
 
+
     @pl.when(section == 0)
     def _():
         for b in range(batches):
-            in_grad[b] = fb[b, 0]
-            for to in range(1, 4):
-                final_copy(b, to).wait_send()
+            deliver(b, fb[b, 0])
+        await_bytes(fb.at[0:3], fin_send.at[0])
+
+    await_bytes(ob.at[1], ring_send.at[1])
+
+    @pl.when(section != 0)
+    def _():
+        await_bytes(ob.at[0], ring_send.at[0])
+
+    for lap in (1, 0):
+        for k in range(3):
+            pair_copy(lap, k).wait_send()
+            await_bytes(st[k].at[lap, 0 : chips - 1], plane_send.at[k, lap])
+
+    collect(0, 2)
 
     @pl.when(section != 0)
     def _():
         for b in range(batches):
             final_copy(b, section).wait_recv()
-            in_grad[b] = frx[b]
-
-    def ring_left(i, carry):
-        lap = 1 - i // batches
-
-        @pl.when((section != 0) | (lap == 1))
-        def _():
-            for k in range(3):
-                ring_copy(lap, lax.rem(i, batches), k).wait_send()
-
-        return carry
-
-    lax.fori_loop(0, 2 * batches, ring_left, 0)
-    for lap in (1, 0):
-        for k in range(3):
-            pair_copy(lap, k).wait_send()
-
-            def left(off, carry):
-                plane_copy(lap, k, lax.rem(chip + off, chips)).wait_send()
-                return carry
-
-            lax.fori_loop(1, chips, left, 0)
-    collect(0, 2)
+            deliver(b, frx[b])
 
 
 def body(n_dp, h_saved, out_cot, so2_weight, radial, edge_angle, edge_atoms, edge_count, atom_count):
@@ -521,13 +545,14 @@
     in_grad, wout = pl.pallas_call(
         functools.partial(kernel, n_dp, scale),
         out_shape=(
-            jax.ShapeDtypeStruct((batches, 2, 32, channels), BF16),
-            jax.ShapeDtypeStruct((2, 5, share, channels), F32),
+            pltpu.VMEM((batches, coeff_rows, 2, channels), BF16),
+            pltpu.VMEM((2, 5, share, 1, channels), F32),
         ),
         in_specs=[pl.BlockSpec(memory_space=pl.ANY)] * 8,
         out_specs=(vmem, vmem),
         scratch_shapes=homes
         + [
+            pltpu.VMEM((2, 5 * channels, channels), BF16),
             pltpu.VMEM((2, 2 * batches, edges), F32),
             pltpu.VMEM((batches, 5, 8, 8, channels), F32),
             pltpu.VMEM((batches, 5, 8, 8, channels), F32),
@@ -543,12 +568,13 @@
             pltpu.VMEM((2, batches, ROWS[1], 2 * channels), BF16),
             pltpu.VMEM((2, batches, ROWS[2], channels), BF16),
         ]
-        + [pltpu.VMEM((slots, r, channels), BF16) for r in ROWS]
-        + [pltpu.VMEM((slots, r, channels), BF16) for r in ROWS]
+        + [pltpu.VMEM((slots, r, channels), BF16) for r in UNIT_ROWS]
         + [
+            pltpu.VMEM((2, batches * sum(UNIT_ROWS), channels), BF16),
             pltpu.VMEM((channels // LANES, 152, LANES), F32),
-            pltpu.VMEM((batches, 4, 2, 32, channels), BF16),
-            pltpu.VMEM((batches, 2, 32, channels), BF16),
+            pltpu.VMEM((channels // LANES, 48, LANES), F32),
+            pltpu.VMEM((batches, 4, 48, channels), BF16),
+            pltpu.VMEM((batches, 48, channels), BF16),
             pltpu.VMEM((2, channels, channels), F32),
         ]
         + [pltpu.VMEM((2, 2, chips, 16, n), BF16) for n in WIDE]
@@ -557,22 +583,21 @@
         + [pltpu.VMEM((2, chips, 16, n), BF16) for n in WIDE]
         + [
             dma((10,)),
-            dma((3, slots)),
-            dma((3, slots)),
-            dma((batches, 4)),
+            dma((2,)),
+            dma((len(UNITS), slots)),
+            dma((1,)),
             dma((batches,)),
             dma((3, 2)),
             dma((3, 2)),
-            dma((3, 2, chips)),
-            dma((3, 2, chips)),
+            dma((3, 2)),
+            dma((3, 2)),
         ],
         compiler_params=pltpu.CompilerParams(
             collective_id=0, has_side_effects=True, vmem_limit_bytes=60 * 1024 * 1024
         ),
         name="window_backward",
     )(*args)
-    in_grad = in_grad[:, :, :coeff_rows]
-    return in_grad, wout[:, None]
+    return in_grad.transpose(0, 2, 1, 3), wout.transpose(0, 3, 1, 2, 4)
 
 
 def solution(mesh):

time: 60 us -> 54.9 us (0.915)
  Pallas kernels: 55.7 us -> 52.8 us
  local copies, waits for them, and re-layouts: 3.48 us -> 1.32 us
    pallas_call x1, Pallas kernels: 55.7 us -> 52.8 us  [body(): pl.pallas_call(functools.partial(kernel, n_dp, scale), out_shape=(pltpu.V...]
    unnamed x2, local copies, waits for them, and re-layouts: 2.54 us -> 1.32 us
    slice x1 -> x0, local copies, waits for them, and re-layouts: 0.93 us -> none  [body(): in_grad = in_grad[:, :, :coeff_rows]]
where the time goes in v3:
time: 54.9 us; the launch traced here: 54.8 us
  Pallas kernels  52.8 us (96%)
  local copies, waits for them, and re-layouts  1.32 us (2%)
  between operations  0.64 us (1%)
    pallas_call x1, Pallas kernels, body(): pl.pallas_call(functools.partial(kernel, n_dp, scale), out_shape=(pltpu.V...  52.8 us
    unnamed x2, local copies, waits for them, and re-layouts  1.32 us

profile of v3, /device:TPU:1, one launch (start us, length us, event | category | flops | bytes accessed | tf_op | source)
XLA Modules:
  0.0 54.8 jit_solution(6482080173998537474)
XLA Ops:
  0.6 52.8 %window_backward.1 = (bf16[4,19,2,384]{3,2,1,0:T(2,128)(2,1)S(1)}, f32[2,5,12,1,384]{4,3,2,1,0:T(1,128)S(1)}) custom-call(bf16[2,4,19,8,384]{4,3,2,1,0:T(8,128)(2,1)} %bitcast.10, bf16[4,19,8,384]{3,2,1,0:T(8,128)(2,1)} %bitcast.11, bf16[2,5,384,384]{3,2,1,0:T(8,128)(2,1)} %bitcast.9, bf16[4,112,384]{2,1,0:T(8,128)(2,1)} %radial_in.1, f32[4,112]{1,0:T(4,128)} %angle_in.1, ...), custom_call_target="tpu_custom_call" | custom-call | tf_op jit(solution)/shard_map/window_backward/pallas_call | solution.py:545
  53.5 0.6 %copy.12 = bf16[4,2,19,384]{3,1,2,0:T(2,128)(2,1)} copy(bf16[4,2,19,384]{3,1,2,0:T(2,128)(2,1)S(1)} %bitcast.8) | data formatting | bytes 233472
  54.1 0.7 %copy.13 = f32[2,1,5,12,384]{4,1,3,2,0:T(1,128)} copy(f32[2,1,5,12,384]{4,1,3,2,0:T(1,128)S(1)} %bitcast.7) | data formatting | bytes 368640

commit v4 on v3

--- a/solution.py
+++ b/solution.py
@@ -68,12 +68,13 @@
     h, g0, w, radial, angle, atoms, ecount, acount,
     wt, trig, tab_f, tab_b, hs1, hs2, hs0, y, summed, gates, sums, dref, ub1, ub2, ub0,
     rb_0, rb_1, rb_2, rb_3, rb_4, rb_5, ob, fx, fy, fb, frx, dwf,
-    pk1, pk2, pk0, px1, px2, px0, st1, st2, st0, rs1, rs2, rs0,
+    hx1, hx2, hx0, ux1, ux2, ux0, pk1, pk2, pk0, rs1, rs2, rs0,
     in_sem, ring_send, ring_recv, fin_send, fin_recv, pair_send, pair_recv, plane_send, plane_recv,
 ):
     hs, ub = (hs1, hs2, hs0), (ub1, ub2, ub0)
     rb = (rb_0, rb_1, rb_2, rb_3, rb_4, rb_5)
-    pk, px, st, rs = (pk1, pk2, pk0), (px1, px2, px0), (st1, st2, st0), (rs1, rs2, rs0)
+    hx, ux = (hx1, hx2, hx0), (ux1, ux2, ux0)
+    pk, rs = (pk1, pk2, pk0), (rs1, rs2, rs0)
     batches, coeff_rows, atom_slots, channels = g0.shape
     edges = angle.shape[1]
     section = lax.axis_index("section")
@@ -149,8 +150,8 @@
                 parts.append(-row.astype(F32) if k < 0 else row.astype(F32))
         return jnp.concatenate(parts, 0)
 
-    def turn_weights(lap):
-        for n in range(5):
+    def turn_weights(lap, slots):
+        for n in slots:
             wt[lap, channels * n : channels * (n + 1)] = w[lap, n].T
 
     def prepare(p):
@@ -165,10 +166,7 @@
         def _():
             inputs[4].wait()
             inputs[5].wait()
-            turn_weights(1)
-            inputs[7].wait()
-            inputs[8].wait()
-            turn_weights(0)
+            turn_weights(1, (1, 2))
 
         h0 = picked(h, lap, b, COEFFS[2][0] + (None,) + COEFFS[2][1]).astype(BF16)
         hs0[lap, b] = h0
@@ -292,6 +290,9 @@
                 later = pl.ds(channels + LANES * j, LANES)
                 ub[k][lap, b, rows, lanes] = jnp.concatenate([up, um], 0).astype(BF16)
                 ub[k][lap, b, rows, later] = jnp.concatenate([um, -up], 0).astype(BF16)
+        if m == 1:
+            for copy in pair_copies(lap, b, k):
+                copy.start()
         first_slot, n_slots = SLOTS[k][0], len(SLOTS[k])
         weight = wt[lap, channels * first_slot : channels * (first_slot + n_slots)]
         out = rb[u][slot].astype(F32) + dot(ub[k][lap, b, rows], weight)
@@ -324,56 +325,25 @@
         for k in range(coeff_rows):
             in_grad[b, k] = v[2 * k : 2 * k + 2].astype(BF16)
 
-    def pair_copy(lap, k):
-        return pltpu.make_async_remote_copy(
-            src_ref=pk[k].at[lap, 1 - core],
-            dst_ref=px[k].at[lap],
-            send_sem=pair_send.at[k, lap],
-            recv_sem=pair_recv.at[k, lap],
-            device_id=(section, dp + 1 - 2 * core),
-            device_id_type=MESH,
-        )
-
-    def weight_term(lap, k):
-        left = hs[k][lap].reshape(batches * ROWS[k], channels)
-        right = ub[k][lap].reshape(batches * ROWS[k], -1)
-        grads = dot_tn(left, right)
-        for n in range(len(SLOTS[k])):
-            dwf[n] = grads[:, channels * n : channels * (n + 1)]
-        low = lax.broadcasted_iota(jnp.int32, (8, channels), 0) < 4
-
-        def pack(j, carry):
-            t = [
-                [dwf[n, pl.ds(pl.multiple_of(24 * j + 8 * i, 8), 8), :] for i in range(3)]
-                for n in range(len(SLOTS[k]))
-            ]
-            if k == 2:
-                blocks = (
-                    jnp.concatenate([t[0][0], t[0][1]], 0),
-                    jnp.concatenate([t[0][2], pltpu.roll(t[0][1], 4, 0)], 0),
-                )
-            else:
-                blocks = []
-                for c in range(2):
-                    if c == 0:
-                        mixed = jnp.where(low, t[0][1], pltpu.roll(t[1][1], 4, 0))
-                    else:
-                        mixed = jnp.where(low, pltpu.roll(t[0][1], 4, 0), t[1][1])
-                    whole = jnp.concatenate([t[0][2 * c], t[1][2 * c]], 0)
-                    last = jnp.concatenate([mixed[:, 256:], jnp.zeros((8, LANES), F32)], 1)
-                    blocks.append(
-                        jnp.concatenate([whole, jnp.concatenate([mixed[:, :256], last], 0)], 1)
-                    )
-            for c in range(2):
-                pk[k][lap, c, j] = blocks[c].astype(BF16)
-            return carry
-
-        lax.fori_loop(0, chips, pack, 0, unroll=min(4, chips))
-        pair_copy(lap, k).start()
+    def pair_copies(lap, b, k):
+        return [
+            pltpu.make_async_remote_copy(
+                src_ref=src[k].at[lap, b],
+                dst_ref=dst[k].at[lap, b],
+                send_sem=pair_send.at[n, k, lap],
+                recv_sem=pair_recv.at[n, k, lap],
+                device_id=(section, dp + 1 - 2 * core),
+                device_id_type=MESH,
+            )
+            for n, (src, dst) in enumerate(((hs, hx), (ub, ux)))
+        ]
+
+    def await_bytes(ref, sem):
+        pltpu.make_async_copy(ref, ref, sem).wait()
 
     def plane_copy(lap, k, to):
         return pltpu.make_async_remote_copy(
-            src_ref=st[k].at[lap, to],
+            src_ref=pk[k].at[lap, to],
             dst_ref=rs[k].at[lap, chip],
             send_sem=plane_send.at[k, lap],
             recv_sem=plane_recv.at[k, lap],
@@ -381,21 +351,42 @@
             device_id_type=MESH,
         )
 
-    def await_bytes(ref, sem):
-        pltpu.make_async_copy(ref, ref, sem).wait()
-
-    def spread(lap, k):
-        pair_copy(lap, k).wait_recv()
-
-        def add(off, carry):
+    def weight_term(lap, k):
+        def product(left, right):
+            rows = batches * ROWS[k]
+            return dot_tn(left[k][lap].reshape(rows, channels), right[k][lap].reshape(rows, -1))
+
+        grads = product(hs, ub)
+        await_bytes(hx[k].at[lap], pair_recv.at[0, k, lap])
+        await_bytes(ux[k].at[lap], pair_recv.at[1, k, lap])
+        grads = grads + product(hx, ux)
+        for n in range(len(SLOTS[k])):
+            dwf[n] = grads[:, channels * n : channels * (n + 1)]
+        low = lax.broadcasted_iota(jnp.int32, (8, channels), 0) < 4
+
+        def rows_of(n, start):
+            return dwf[n, pl.ds(pl.multiple_of(start, 8), 8), :]
+
+        def block(j):
+            whole = [rows_of(n, 24 * j + 16 * core) for n in range(len(SLOTS[k]))]
+            middle = [rows_of(n, 24 * j + 8) for n in range(len(SLOTS[k]))]
+            raised = jnp.where(core == 0, middle[0], pltpu.roll(middle[0], 4, 0))
+            if k == 2:
+                return jnp.concatenate([whole[0], raised], 0).astype(BF16)
+            lowered = jnp.where(core == 0, pltpu.roll(middle[1], 4, 0), middle[1])
+            mixed = jnp.where(low, raised, lowered)
+            last = jnp.concatenate([mixed[:, 256:], jnp.zeros((8, LANES), F32)], 1)
+            side = jnp.concatenate([mixed[:, :256], last], 0)
+            return jnp.concatenate([jnp.concatenate(whole, 0), side], 1).astype(BF16)
+
+        def pack(off, carry):
             j = lax.rem(chip + off, chips)
-            st[k][lap, j] = (pk[k][lap, core, j].astype(F32) + px[k][lap, j].astype(F32)).astype(BF16)
+            pk[k][lap, j] = block(j)
             plane_copy(lap, k, j).start()
             return carry
 
-        lax.fori_loop(1, chips, add, 0, unroll=min(5, chips - 1))
-        own = (pk[k][lap, core, chip].astype(F32) + px[k][lap, chip].astype(F32)).astype(BF16)
-        rs[k][lap, chip] = own
+        lax.fori_loop(1, chips, pack, 0, unroll=min(5, chips - 1))
+        rs[k][lap, chip] = block(chip)
 
     def collect(lap, k):
         await_bytes(rs[k].at[lap, 0 : chips - 1], plane_recv.at[k, lap])
@@ -436,8 +427,18 @@
 
         lax.fori_loop(lo, hi, one, 0)
 
-    ahead = jnp.where(section == 3, 2, jnp.where(section == 2, batches, 2 * batches))
-    prepare_range(0, ahead)
+    prepare_range(0, jnp.where(section == 3, 1, batches))
+
+    def turn_rest():
+        turn_weights(1, (3, 4, 0))
+        inputs[7].wait()
+        inputs[8].wait()
+        turn_weights(0, range(5))
+
+    @pl.when(section != 3)
+    def _():
+        turn_rest()
+
     inputs[6].wait()
     inputs[9].wait()
     pl.semaphore_wait(barrier, 4 + chips - 1)
@@ -448,8 +449,10 @@
         def first(b, carry):
             now = jnp.where(section == 3, batches * turn_index + b, batches)
             until = jnp.where(section == 3, now + 1, batches + batches)
-            late = (section == 3) & (lap == 1) & (b >= 2)
+            late = (section == 3) & (lap == 1) & (b >= 1)
             fill = (section >= 2) & (lap == 0) & (b == 0)
+            early = (section < 2) & (lap == 1) & (b == 0)
+            fill = fill | early
             lo = jnp.where(fill, batches, now)
             hi = jnp.where(fill, 2 * batches, jnp.where(late, until, lo))
             prepare_range(lo, hi)
@@ -458,20 +461,24 @@
             return carry
 
         lax.fori_loop(0, batches, first, 0)
-        weight_term(lap, 0)
+
+        @pl.when((section == 3) & (lap == 1))
+        def _():
+            turn_rest()
+
+        now = (section != 3) | (lap == 0)
 
         def second(b, carry):
             unit(lap, b, 2)
             unit(lap, b, 3)
 
-            @pl.when(b == 1)
+            @pl.when((b == 1) & now)
             def _():
-                spread(lap, 0)
+                weight_term(lap, 0)
 
             return carry
 
         lax.fori_loop(0, batches, second, 0)
-        weight_term(lap, 1)
 
         def third(b, carry):
             unit(lap, b, 4)
@@ -481,23 +488,31 @@
             def _():
                 finish(b)
 
-            @pl.when(b == 1)
+            @pl.when((b == 1) & now)
             def _():
-                spread(lap, 1)
+                weight_term(lap, 1)
 
             return carry
 
         lax.fori_loop(0, batches, third, 0)
-        weight_term(lap, 2)
+
+        @pl.when(now)
+        def _():
+            weight_term(lap, 2)
 
         @pl.when((section == 0) & (lap == 0))
         def _():
             finish(batches - 1)
 
-        spread(lap, 2)
         return carry
 
     lax.fori_loop(0, 2, run_lap, 0)
+
+    @pl.when(section == 3)
+    def _():
+        for k in range(3):
+            weight_term(1, k)
+
     for lap, k in ((1, 0), (1, 1), (1, 2), (0, 0), (0, 1)):
         collect(lap, k)
 
@@ -516,8 +531,9 @@
 
     for lap in (1, 0):
         for k in range(3):
-            pair_copy(lap, k).wait_send()
-            await_bytes(st[k].at[lap, 0 : chips - 1], plane_send.at[k, lap])
+            await_bytes(hs[k].at[lap], pair_send.at[0, k, lap])
+            await_bytes(ub[k].at[lap], pair_send.at[1, k, lap])
+            await_bytes(pk[k].at[lap, 0 : chips - 1], plane_send.at[k, lap])
 
     collect(0, 2)
 
@@ -577,8 +593,12 @@
             pltpu.VMEM((batches, 48, channels), BF16),
             pltpu.VMEM((2, channels, channels), F32),
         ]
-        + [pltpu.VMEM((2, 2, chips, 16, n), BF16) for n in WIDE]
-        + [pltpu.VMEM((2, chips, 16, n), BF16) for n in WIDE]
+        + [pltpu.VMEM((2, batches, r, channels), BF16) for r in ROWS]
+        + [
+            pltpu.VMEM((2, batches, ROWS[0], 2 * channels), BF16),
+            pltpu.VMEM((2, batches, ROWS[1], 2 * channels), BF16),
+            pltpu.VMEM((2, batches, ROWS[2], channels), BF16),
+        ]
         + [pltpu.VMEM((2, chips, 16, n), BF16) for n in WIDE]
         + [pltpu.VMEM((2, chips, 16, n), BF16) for n in WIDE]
         + [
@@ -587,8 +607,8 @@
             dma((len(UNITS), slots)),
             dma((1,)),
             dma((batches,)),
-            dma((3, 2)),
-            dma((3, 2)),
+            dma((2, 3, 2)),
+            dma((2, 3, 2)),
             dma((3, 2)),
             dma((3, 2)),
         ],

time: 54.9 us -> 53.8 us (0.980)
  Pallas kernels: 52.8 us -> 51.8 us
    pallas_call x1, Pallas kernels: 52.8 us -> 51.8 us  [body(): pl.pallas_call(functools.partial(kernel, n_dp, scale), out_shape=(pltpu.V...]
where the time goes in v4:
time: 53.8 us; the launch traced here: 53.7 us
  Pallas kernels  51.8 us (96%)
  local copies, waits for them, and re-layouts  1.32 us (2%)
  between operations  0.64 us (1%)
    pallas_call x1, Pallas kernels, body(): pl.pallas_call(functools.partial(kernel, n_dp, scale), out_shape=(pltpu.V...  51.8 us
    unnamed x2, local copies, waits for them, and re-layouts  1.32 us

profile of v4, /device:TPU:1, one launch (start us, length us, event | category | flops | bytes accessed | tf_op | source)
XLA Modules:
  0.0 53.7 jit_solution(4029344739894011715)
XLA Ops:
  0.6 51.8 %window_backward.1 = (bf16[4,19,2,384]{3,2,1,0:T(2,128)(2,1)S(1)}, f32[2,5,12,1,384]{4,3,2,1,0:T(1,128)S(1)}) custom-call(bf16[2,4,19,8,384]{4,3,2,1,0:T(8,128)(2,1)} %bitcast.10, bf16[4,19,8,384]{3,2,1,0:T(8,128)(2,1)} %bitcast.11, bf16[2,5,384,384]{3,2,1,0:T(8,128)(2,1)} %bitcast.9, bf16[4,112,384]{2,1,0:T(8,128)(2,1)} %radial_in.1, f32[4,112]{1,0:T(4,128)} %angle_in.1, ...), custom_call_target="tpu_custom_call" | custom-call | tf_op jit(solution)/shard_map/window_backward/pallas_call | solution.py:561
  52.4 0.6 %copy.12 = bf16[4,2,19,384]{3,1,2,0:T(2,128)(2,1)} copy(bf16[4,2,19,384]{3,1,2,0:T(2,128)(2,1)S(1)} %bitcast.8) | data formatting | bytes 233472
  53.1 0.7 %copy.13 = f32[2,1,5,12,384]{4,1,3,2,0:T(1,128)} copy(f32[2,1,5,12,384]{4,1,3,2,0:T(1,128)S(1)} %bitcast.7) | data formatting | bytes 368640

commit v5 on v4

--- a/solution.py
+++ b/solution.py
@@ -290,9 +290,6 @@
                 later = pl.ds(channels + LANES * j, LANES)
                 ub[k][lap, b, rows, lanes] = jnp.concatenate([up, um], 0).astype(BF16)
                 ub[k][lap, b, rows, later] = jnp.concatenate([um, -up], 0).astype(BF16)
-        if m == 1:
-            for copy in pair_copies(lap, b, k):
-                copy.start()
         first_slot, n_slots = SLOTS[k][0], len(SLOTS[k])
         weight = wt[lap, channels * first_slot : channels * (first_slot + n_slots)]
         out = rb[u][slot].astype(F32) + dot(ub[k][lap, b, rows], weight)
@@ -301,6 +298,10 @@
         @pl.when((section != 0) | (lap == 1))
         def _():
             ring_copy(lap, b, u).start()
+
+        if m == 1:
+            for copy in pair_copies(lap, b, k):
+                copy.start()
 
     def finish(b):
         for j, lanes in enumerate(tiles):
@@ -450,8 +451,8 @@
             now = jnp.where(section == 3, batches * turn_index + b, batches)
             until = jnp.where(section == 3, now + 1, batches + batches)
             late = (section == 3) & (lap == 1) & (b >= 1)
-            fill = (section >= 2) & (lap == 0) & (b == 0)
-            early = (section < 2) & (lap == 1) & (b == 0)
+            fill = (section == 3) & (lap == 0) & (b == 0)
+            early = (section != 3) & (lap == 1) & (b == 0)
             fill = fill | early
             lo = jnp.where(fill, batches, now)
             hi = jnp.where(fill, 2 * batches, jnp.where(late, until, lo))
@@ -467,12 +468,13 @@
             turn_rest()
 
         now = (section != 3) | (lap == 0)
+        soon = jnp.where((section == 0) & (lap == 0), 0, 1)
 
         def second(b, carry):
             unit(lap, b, 2)
             unit(lap, b, 3)
 
-            @pl.when((b == 1) & now)
+            @pl.when((b == soon) & now)
             def _():
                 weight_term(lap, 0)
 
@@ -488,7 +490,7 @@
             def _():
                 finish(b)
 
-            @pl.when((b == 1) & now)
+            @pl.when((b == soon) & now)
             def _():
                 weight_term(lap, 1)
 

time: 53.8 us -> 53.9 us (level)
  no operation moved by 1% of the time
where the time goes in v5:
time: 53.9 us; the launch traced here: 53.8 us
  Pallas kernels  51.9 us (96%)
  local copies, waits for them, and re-layouts  1.32 us (2%)
  between operations  0.64 us (1%)
    pallas_call x1, Pallas kernels, body(): pl.pallas_call(functools.partial(kernel, n_dp, scale), out_shape=(pltpu.V...  51.9 us
    unnamed x2, local copies, waits for them, and re-layouts  1.32 us

profile of v5, /device:TPU:1, one launch (start us, length us, event | category | flops | bytes accessed | tf_op | source)
XLA Modules:
  0.0 53.8 jit_solution(3880184599679117855)
XLA Ops:
  0.6 51.9 %window_backward.1 = (bf16[4,19,2,384]{3,2,1,0:T(2,128)(2,1)S(1)}, f32[2,5,12,1,384]{4,3,2,1,0:T(1,128)S(1)}) custom-call(bf16[2,4,19,8,384]{4,3,2,1,0:T(8,128)(2,1)} %bitcast.10, bf16[4,19,8,384]{3,2,1,0:T(8,128)(2,1)} %bitcast.11, bf16[2,5,384,384]{3,2,1,0:T(8,128)(2,1)} %bitcast.9, bf16[4,112,384]{2,1,0:T(8,128)(2,1)} %radial_in.1, f32[4,112]{1,0:T(4,128)} %angle_in.1, ...), custom_call_target="tpu_custom_call" | custom-call | tf_op jit(solution)/shard_map/window_backward/pallas_call | solution.py:563
  52.5 0.6 %copy.12 = bf16[4,2,19,384]{3,1,2,0:T(2,128)(2,1)} copy(bf16[4,2,19,384]{3,1,2,0:T(2,128)(2,1)S(1)} %bitcast.8) | data formatting | bytes 233472
  53.1 0.7 %copy.13 = f32[2,1,5,12,384]{4,1,3,2,0:T(1,128)} copy(f32[2,1,5,12,384]{4,1,3,2,0:T(1,128)S(1)} %bitcast.7) | data formatting | bytes 368640
